TPU v7x, 256 devices: a whole 4x4x8 slice. The times are simulated.
256 devices in a mesh: dp: 64 (over z, y, core), mp: 4 (over x).
Axes of the slice: x: 4, y: 4, z: 8, core: 2. Of those that a mesh axis runs over, the one named last changes fastest.
Arguments:
- activations: bfloat16 [32768, 3072], P('dp', 'mp'), may hold values from -16 to 16
- cotangent: bfloat16 [32768, 6144], P('dp', 'mp'), may hold values from -6 to 6
- block_owner: int32 [72], replicated, may hold values from 0 to 63, as said below
- left_factor: float32 [128, 1024, 256], P('dp', 'mp'), as said below
- right_factor: float32 [128, 1024, 256], P('dp', 'mp'), as said below
- left_basis: float32 [128, 1024, 256], P('dp', 'mp')
- right_basis: float32 [128, 1024, 256], P('dp', 'mp')
Outputs:
- update: bfloat16 [256, 12, 6144], P('dp', None, 'mp')
- left_next: float32 [128, 1024, 256], P('dp', 'mp')
- right_next: float32 [128, 1024, 256], P('dp', 'mp')
- left_basis_next: float32 [128, 1024, 256], P('dp', 'mp')
- right_basis_next: float32 [128, 1024, 256], P('dp', 'mp')
Inputs may be any that keep to these rules, and one draw needn't show every extreme that they name: Block b is held by dp index block_owner[b]; every dp index holds 1 or 2 blocks, so at most 2. `left_factor`: every 256 x 256 block is symmetric positive definite. `right_factor`: every 256 x 256 block is symmetric positive definite.
All inputs are finite; a program needn't handle non-finite values.
Results may differ from a plain program's by a relative error of at most 0.001.
Values may be sent and summed in bfloat16 or wider, within the bound.
A program may use at most 256 MiB of HBM per device.

v0:
```python
import math

import jax
import jax.numpy as jnp
from jax import lax
from jax.sharding import PartitionSpec as P

NSTEPS = 6


BETA = 0.9
EPS = 1e-06
HIGHEST = lax.Precision.HIGHEST


def product(left_side, right_side):
    return jnp.dot(left_side, right_side, precision=HIGHEST, preferred_element_type=jnp.float32)


def slot_numbers(block_owner, capacity):
    positions = jnp.arange(block_owner.shape[0], dtype=jnp.int32)
    same_owner = block_owner[:, None] == block_owner[None, :]
    earlier = positions[None, :] < positions[:, None]
    slot_rank = jnp.sum(jnp.where(same_owner & earlier, 1, 0), axis=1).astype(jnp.int32)
    return block_owner * capacity + slot_rank


def orthogonalize(matrix):
    current = matrix / jnp.sqrt(jnp.sum(matrix * matrix) + EPS)
    identity = jnp.eye(matrix.shape[0], dtype=jnp.float32)
    for _ in range(NSTEPS):
        current = product(current, 1.5 * identity - 0.5 * product(current.T, current))
    return current


def refresh(gradient, left_old, right_old, left_prev, right_prev):
    order_size = gradient.shape[0]
    left_new = BETA * left_old + (1.0 - BETA) / order_size * product(gradient, gradient.T)
    right_new = BETA * right_old + (1.0 - BETA) / order_size * product(gradient.T, gradient)
    left_power = product(left_new, left_prev)
    right_power = product(right_new, right_prev)
    left_fresh = orthogonalize(left_power)
    right_fresh = orthogonalize(right_power)
    left_scale = (jnp.mean(left_power * left_power, axis=0) + EPS) ** (-0.125)
    right_scale = (jnp.mean(right_power * right_power, axis=0) + EPS) ** (-0.125)
    rotated = product(product(left_fresh.T, gradient), right_fresh)
    rotated = rotated * left_scale[:, None] * right_scale[None, :]
    block_update = product(product(left_fresh, rotated), right_fresh.T).astype(jnp.bfloat16)
    return (block_update, left_new, right_new, left_fresh, right_fresh)


def on_device(
    activations, cotangent, block_owner, left_factor, right_factor, left_basis, right_basis
):
    dp_count = lax.axis_size("dp")
    capacity = left_factor.shape[0]
    block_size = left_factor.shape[2]
    local_tokens = activations.shape[0]
    gathered = lax.all_gather(activations, "mp", axis=1, tiled=True)
    bands = gathered.shape[1] // block_size
    columns = cotangent.shape[1]
    col_blocks = columns // block_size
    block_count = bands * col_blocks
    token_scale = 1.0 / math.sqrt(local_tokens * dp_count)
    banded = gathered.reshape(local_tokens, bands, block_size)
    slot_ids = slot_numbers(block_owner, capacity)
    slot_range = jnp.arange(dp_count * capacity, dtype=jnp.int32)
    matches = slot_ids[None, :] == slot_range[:, None]
    occupied = jnp.any(matches, axis=1)
    block_range = jnp.arange(block_count, dtype=jnp.int32)
    source_block = jnp.sum(jnp.where(matches, block_range[None, :], 0), axis=1)
    partial_value = jnp.einsum("tir,tc->ric", banded, cotangent, preferred_element_type=jnp.float32)
    summed = lax.psum_scatter(partial_value * token_scale, "dp", scatter_dimension=0, tiled=True)
    outgoing_rows = jnp.take(
        summed.reshape(summed.shape[0], block_count, block_size), source_block, axis=1
    )
    outgoing_rows = jnp.where(occupied[None, :, None], outgoing_rows, 0.0)
    arrived = lax.all_to_all(outgoing_rows, "dp", split_axis=1, concat_axis=0, tiled=True)
    owned_blocks = jnp.swapaxes(arrived, 0, 1)
    own_index = lax.axis_index("dp")
    live_here = lax.dynamic_slice_in_dim(occupied, own_index * capacity, capacity, 0)

    def handle_slot(unused_carry, slot_entry):
        is_live = slot_entry[0]
        operands = slot_entry[1:]

        def refresh_slot(values):
            return refresh(*values)

        def skip_slot(values):
            return (
                jnp.zeros(values[0].shape, jnp.bfloat16),
                values[1],
                values[2],
                values[3],
                values[4],
            )

        return (unused_carry, lax.cond(is_live, refresh_slot, skip_slot, operands))

    _, results = lax.scan(
        handle_slot,
        jnp.zeros((), jnp.int32),
        (live_here, owned_blocks, left_factor, right_factor, left_basis, right_basis),
    )
    updates, left_next, right_next, left_basis_next, right_basis_next = results
    outgoing = jnp.swapaxes(updates, 0, 1)
    returned = lax.all_to_all(outgoing, "dp", split_axis=0, concat_axis=1, tiled=True)
    own_rows = jnp.take(returned, slot_ids, axis=1)
    update = own_rows.reshape(own_rows.shape[0], bands, columns)
    return (update, left_next, right_next, left_basis_next, right_basis_next)


def solution(mesh):
    placed = (
        P("dp", "mp"),
        P("dp", "mp"),
        P(),
        P("dp", "mp", None),
        P("dp", "mp", None),
        P("dp", "mp", None),
        P("dp", "mp", None),
    )
    return jax.shard_map(
        on_device,
        mesh=mesh,
        in_specs=placed,
        out_specs=(
            P("dp", None, "mp"),
            P("dp", "mp", None),
            P("dp", "mp", None),
            P("dp", "mp", None),
            P("dp", "mp", None),
        ),
        check_vma=False,
    )
```

profile of v0, /device:TPU:1, one launch (start us, length us, event | category | flops | bytes accessed | tf_op | source)
XLA Modules:
  0.0 430.5 jit_solution(1836968402683989302)
XLA Ops:
  7.2 2.4 copy.40
  9.7 46.0 %all-gather.2.cloned.1.call-done = bf16[512,3072]{0,1:T(8,128)(2,1)} async-done(((bf16[512,768]{0,1:T(8,128)(2,1)}), bf16[512,3072]{0,1:T(8,128)(2,1)}) %all-gather.2.cloned.1.call-update) | async-done | bytes 3145744 | tf_op jit(solution)/shard_map/all_gather | solution.py:59
  55.7 11.0 %multiply_bitcast_fusion = f32[256,12,1536]{0,2,1:T(8,128)} fusion(bf16[512,12,256]{0,2,1:T(8,128)(2,1)} %bitcast.130, bf16[512,1536]{1,0:T(8,128)(2,1)S(1)} %copy-done), kind=kOutput, calls=%fused_computation.64 | convolution fusion | flops 4836556800 | bytes 23592960 | tf_op jit(solution)/shard_map/tir,tc->ric/dot_general | solution.py:72
  66.7 22.6 %copy.43 = f32[256,12,1536]{2,1,0:T(8,128)} copy(f32[256,12,1536]{0,2,1:T(8,128)} %multiply_bitcast_fusion) | data formatting | bytes 37748736 | tf_op jit(solution)/shard_map/mul | solution.py:73
  90.5 215.8 %reduce-scatter.2.cloned.1.call-done = f32[4,12,1536]{2,1,0:T(8,128)} async-done(((f32[256,12,1536]{2,1,0:T(8,128)}), f32[4,12,1536]{2,1,0:T(8,128)}) %reduce-scatter.2.cloned.1.call-update) | async-done | bytes 294928 | tf_op jit(solution)/shard_map/reduce_scatter | solution.py:73
  306.2 1.1 reshape.62
  307.4 0.9 gather_fusion
  308.3 1.1 select_bitcast_fusion
  309.4 11.8 %all-to-all-start = ((f32[4,128,256]{2,0,1:T(4,128)}), f32[4,128,256]{2,0,1:T(4,128)S(1)}, u32[]{:S(2)}, u32[]{:S(2)}) async-start(f32[4,128,256]{2,0,1:T(4,128)} %select_bitcast_fusion), calls=%async_computation.1 | async-start | bytes 1048576 | tf_op jit(solution)/shard_map/all_to_all | solution.py:78
  321.4 17.6 %all-to-all-done = f32[4,128,256]{2,0,1:T(4,128)S(1)} async-done(((f32[4,128,256]{2,0,1:T(4,128)}), f32[4,128,256]{2,0,1:T(4,128)S(1)}, u32[]{:S(2)}, u32[]{:S(2)}) %all-to-all-start) | async-done | bytes 524320 | tf_op jit(solution)/shard_map/all_to_all | solution.py:78
  339.2 38.0 %while.18 = (s32[]{:T(128)}, bf16[2,256,256]{2,1,0:T(8,128)(2,1)S(1)}, f32[2,256,256]{2,1,0:T(8,128)}, f32[2,256,256]{2,1,0:T(8,128)}, f32[2,256,256]{2,1,0:T(8,...) while((s32[]{:T(128)}, ...), condition=%wide.region_11.12_spmd, body=%wide.region_4.11_spmd.sunk | while | flops 6446842368 | bytes 26355040 | solution.py:101
  339.4 0.7 dynamic-slice_bitcast_fusion.10
  340.1 1.7 dynamic-slice_bitcast_fusion.11
  343.0 25.2 %conditional.2 = (f32[256,256]{1,0:T(8,128)S(1)}, f32[256,256]{1,0:T(8,128)S(1)}, f32[256,256]{1,0:T(8,128)}, f32[256,256]{1,0:T(8,128)}, bf16[1,256,256]{2,1,0:T(8,128)(2,1)S(1)}) conditional(s32[]{:T(128)} %bitcast.122, (f32[256,256]{1,0:T(8,128)S(1)}, f32[256,256]{1,0:T(8,128)S(1)}, f32[256,256]{1,0:T(8,128)}, f32[256,256]{1,0:T(8,128)}) %tuple.52, ...), branch_computations={%region_5.5_spmd, %region_6.10_spmd} | conditional | flops 6446842368 | bytes 21897332 | solution.py:99
  343.7 1.9 multiply_reduce_fusion
  351.8 1.1 fusion.29
  353.4 1.9 multiply_reduce_fusion.2
  361.5 1.1 fusion.24
  362.6 1.5 fusion.4
  364.2 1.3 fusion
  365.5 1.3 fusion.30
  366.8 1.4 fusion.3
  368.2 1.9 bitcast_dynamic-update-slice_fusion.7
  370.1 0.8 bitcast_dynamic-update-slice_fusion.6
  370.9 0.7 dynamic-slice_bitcast_fusion.10
  371.6 1.7 dynamic-slice_bitcast_fusion.11
  374.5 1.9 bitcast_dynamic-update-slice_fusion.7
  376.4 0.8 bitcast_dynamic-update-slice_fusion.6
  377.3 1.0 copy.55
  378.2 30.5 %all-to-all-start.1 = ((bf16[256,2,256]{2,1,0:T(2,128)(2,1)}), bf16[256,2,256]{2,1,0:T(2,128)(2,1)S(1)}, u32[]{:S(2)}, u32[]{:S(2)}) async-start(bf16[256,2,256]{2,1,0:T(2,128)(2,1)} %bitcast.108), calls=%async_computation.2 | async-start | bytes 524288 | tf_op jit(solution)/shard_map/all_to_all | solution.py:108
  408.9 12.9 %all-to-all-done.1 = bf16[256,2,256]{2,1,0:T(2,128)(2,1)S(1)} async-done(((bf16[256,2,256]{2,1,0:T(2,128)(2,1)}), bf16[256,2,256]{2,1,0:T(2,128)(2,1)S(1)}, u32[]{:S(2)}, u32[]{:S(2)}) %all-to-all-start.1) | async-done | bytes 262176 | tf_op jit(solution)/shard_map/all_to_all | solution.py:108
  422.9 0.8 copy.49
  (78 shorter events, 16.3 us)
Async XLA Ops:
  7.2 48.6 %copy-start = (bf16[512,1536]{1,0:T(8,128)(2,1)S(1)}, bf16[512,1536]{1,0:T(8,128)(2,1)}, u32[]{:S(2)}) copy-start(bf16[512,1536]{1,0:T(8,128)(2,1)} %param.12) | copy-start | bytes 4718596
  7.2 48.6 %all-gather.2.cloned.1.call-start = ((), (), s32[]{:S(2)}) async-start(), calls=%async_computation.3 | async-start | bytes 3932160 | tf_op jit(solution)/shard_map/all_gather | solution.py:59
  9.6 296.6 %reduce-scatter.2.cloned.1.call-start = ((), (), s32[]{:S(2)}) async-start(), calls=%async_computation.4 | async-start | bytes 25559040 | tf_op jit(solution)/shard_map/reduce_scatter | solution.py:73
  89.3 0.7 copy-start.5
  90.4 248.8 %copy-start.2 = (f32[2,256,256]{2,1,0:T(8,128)S(1)}, f32[2,256,256]{2,1,0:T(8,128)}, u32[]{:S(2)}) copy-start(f32[2,256,256]{2,1,0:T(8,128)} %param.14) | copy-start | bytes 1572868
  90.4 248.8 %copy-start.3 = (f32[2,256,256]{2,1,0:T(8,128)S(1)}, f32[2,256,256]{2,1,0:T(8,128)}, u32[]{:S(2)}) copy-start(f32[2,256,256]{2,1,0:T(8,128)} %param.15) | copy-start | bytes 1572868
  90.4 248.8 %copy-start.4 = (f32[2,256,256]{2,1,0:T(8,128)S(1)}, f32[2,256,256]{2,1,0:T(8,128)}, u32[]{:S(2)}) copy-start(f32[2,256,256]{2,1,0:T(8,128)} %param.16) | copy-start | bytes 1572868
  309.4 29.5 %all-to-all-start = ((f32[4,128,256]{2,0,1:T(4,128)}), f32[4,128,256]{2,0,1:T(4,128)S(1)}, u32[]{:S(2)}, u32[]{:S(2)}) async-start(f32[4,128,256]{2,0,1:T(4,128)} %select_bitcast_fusion), calls=%async_computation.1 | async-start | bytes 1048576 | tf_op jit(solution)/shard_map/all_to_all | solution.py:78
  377.2 46.4 %copy-start.1 = (bf16[512,1536]{1,0:T(8,128)(2,1)S(1)}, bf16[512,1536]{1,0:T(8,128)(2,1)}, u32[]{:S(2)}) copy-start(bf16[512,1536]{1,0:T(8,128)(2,1)} %param.12) | copy-start | bytes 4718596
  378.2 43.6 %all-to-all-start.1 = ((bf16[256,2,256]{2,1,0:T(2,128)(2,1)}), bf16[256,2,256]{2,1,0:T(2,128)(2,1)S(1)}, u32[]{:S(2)}, u32[]{:S(2)}) async-start(bf16[256,2,256]{2,1,0:T(2,128)(2,1)} %bitcast.108), calls=%async_computation.2 | async-start | bytes 524288 | tf_op jit(solution)/shard_map/all_to_all | solution.py:108
Sparse Core Ops, SparseCore 0:
  9.8 45.8 all-gather.1
  89.5 216.6 reduce-scatter.1
where the time goes:
time: 432 us; the launch traced here: 430 us
  waiting for transfers between devices  292 us (68%)
  local copies, waits for them, and re-layouts  42.4 us (10%)
  starting transfers between devices  42.4 us (10%)
  matrix products  34.7 us (8%)
  between operations  14.3 us (3%)
    reduce_scatter x1, waiting for transfers between devices, on_device(): lax.psum_scatter(partial_value * token_scale, 'dp', scatter_dimension=0,...  216 us
    all_gather x1, waiting for transfers between devices, on_device(): gathered = lax.all_gather(activations, 'mp', axis=1, tiled=True)  46 us
    all_to_all x1, starting transfers between devices, on_device(): lax.all_to_all(outgoing, 'dp', split_axis=0, concat_axis=1, tiled=True)  30.5 us
    dot_general x32, matrix products, product(): jnp.dot(left_side, right_side, precision=HIGHEST, preferred_element_type=...  23.7 us
    mul x1, local copies, waits for them, and re-layouts, on_device(): partial_value * token_scale  22.6 us
    all_to_all x1, waiting for transfers between devices, on_device(): lax.all_to_all(outgoing_rows, 'dp', split_axis=1, concat_axis=0, tiled=True)  17.6 us
    all_to_all x1, waiting for transfers between devices, on_device(): lax.all_to_all(outgoing, 'dp', split_axis=0, concat_axis=1, tiled=True)  12.9 us
    all_to_all x1, starting transfers between devices, on_device(): lax.all_to_all(outgoing_rows, 'dp', split_axis=1, concat_axis=0, tiled=True)  11.8 us
  transfers between devices with their start and end apart: 4, of which 4 were waited for; matrix products, arithmetic and copies ran while one was open for 0% of the time, Pallas kernels for 0%

commit v1 on v0

v1 whole, which is shorter than its diff:
```python
import functools
import math

import jax
import jax.numpy as jnp
from jax import lax
from jax.experimental import pallas as pl
from jax.experimental.pallas import tpu as pltpu
from jax.sharding import PartitionSpec as P

NSTEPS = 6
BETA = 0.9
EPS = 1e-06
HIGHEST = lax.Precision.HIGHEST
MESH = pl.DeviceIdType.MESH
NX, NY, NZ, NQ = 4, 4, 8, 32
BLK = 256
RA, RB = 160, 128
SPARE = 8
PIECES = 6
PROWS = 128


def place():
    dp = lax.axis_index("dp")
    x = lax.axis_index("mp")
    return x, lax.rem(lax.div(dp, 2), NY), lax.div(dp, 2 * NY), lax.rem(dp, 2)


def device(dx=0, dy=0, dz=0, dc=0):
    x, y, z, c = place()
    x = lax.rem(x + dx + NX, NX)
    y = lax.rem(y + dy + NY, NY)
    z = lax.rem(z + dz + NZ, NZ)
    c = lax.rem(c + dc, 2)
    return ((z * NY + y) * 2 + c, x)


def remote(src, dst, send, recv, target):
    return pltpu.make_async_remote_copy(
        src_ref=src, dst_ref=dst, send_sem=send, recv_sem=recv, device_id=target, device_id_type=MESH
    )


def encode(read, groups, dst):
    exponents = []
    for g in range(groups):
        value = read(g)
        top = jnp.max(jnp.abs(value), axis=0, keepdims=True)
        exponent = jnp.ceil(jnp.log2(jnp.maximum(top, 1e-30) * (1.0 / 32700.0)))
        exponents.append(exponent)
        coded = jnp.round(value * jnp.exp2(-exponent))
        dst[pl.ds(16 * g, 16), :] = coded.astype(jnp.int32).astype(jnp.int16)
    exponents.append(jnp.zeros((16 - groups, BLK), jnp.float32))
    tile = jnp.concatenate(exponents, axis=0)
    dst[pl.ds(16 * groups, 16), :] = tile.astype(jnp.int32).astype(jnp.int16)


def decoder(src, groups):
    scales = jnp.exp2(src[pl.ds(16 * groups, 16), :].astype(jnp.int32).astype(jnp.float32))

    def read(g):
        value = src[pl.ds(16 * g, 16), :].astype(jnp.int32).astype(jnp.float32)
        return value * scales[g : g + 1, :]

    return read


def gradient_kernel(
    token_scale,
    owner_ref,
    act_ref,
    cot_ref,
    primary_ref,
    second_ref,
    table_v,
    table_s,
    at,
    cot2,
    part,
    spill,
    ya2_s,
    ya2_r,
    ya1_s,
    ya1_r,
    za4_s,
    za4_r,
    za_s,
    za_r,
    zb4_s,
    zb4_r,
    zb_s,
    zb_r,
    yb2_s,
    yb2_r,
    yb1_s,
    yb1_r,
    sec,
    sec_out,
    sec_in,
    x_send,
    x_recv,
    f_send,
    f_recv,
    c_send,
    c_recv,
    ya2_sem,
    ya1_sem,
    za4_sem,
    za_sem,
    zb4_sem,
    zb_sem,
    yb2_sem,
    yb1_sem,
    t_sem,
    s_sem,
):
    x, y, z, c = place()
    me_q = z * NY + y
    other = device(dc=1)

    barrier = pltpu.get_barrier_semaphore()
    for target in (device(dx=1), device(dx=3), other):
        pl.semaphore_signal(barrier, inc=1, device_id=target, device_id_type=MESH)

    @pl.loop(1, NQ)
    def _(r):
        q = lax.rem(me_q + r, NQ)
        pl.semaphore_signal(barrier, inc=1, device_id=(q * 2 + c, x), device_id_type=MESH)

    def piece(half, shard, p):
        return at.at[half, 3 * shard + p // 2, pl.ds((p % 2) * PROWS, PROWS), :]

    def turn(p):
        at[0, p // 2, pl.ds((p % 2) * PROWS, PROWS), :] = act_ref[:, pl.ds(p * PROWS, PROWS)].T

    order = (0, 5, 1, 4, 2, 3)
    turn(order[0])
    pl.semaphore_wait(barrier, NQ + 2)

    def own_piece(p, d):
        sgn = 1 - 2 * d
        return remote(
            piece(0, 0, p), piece(0, (4 - sgn) % 4, p), x_send.at[d, p], x_recv.at[d, p], device(dx=sgn)
        )

    def forward_piece(p, d):
        sgn = 1 - 2 * d
        return remote(piece(0, (4 - sgn) % 4, p), piece(0, 2, p), f_send.at[p], f_recv.at[p], device(dx=sgn))

    def core_shard(r, sem):
        rows = pl.ds(3 * r, 3)
        return remote(at.at[0, rows], at.at[1, rows], c_send.at[sem], c_recv.at[sem], other)

    def core_piece(p):
        return remote(piece(0, 2, p), piece(1, 2, p), c_send.at[4 + p], c_recv.at[4 + p], other)

    for n, p in enumerate(order):
        if n > 0:
            turn(p)
        own_piece(p, 0).start()
        own_piece(p, 1).start()
    core_shard(0, 1).start()
    for j in range(6):
        cot2[0, j] = cot_ref[:, pl.ds(j * BLK, BLK)]
    cot_copy = remote(cot2.at[0], cot2.at[1], c_send.at[0], c_recv.at[0], other)
    cot_copy.start()

    owners = owner_ref[...]
    lanes = lax.broadcasted_iota(jnp.int32, (128, 128), 1)
    subs = lax.broadcasted_iota(jnp.int32, (128, 128), 0)
    earlier = lanes < subs
    same = jnp.broadcast_to(owners, (128, 128)).T == owners
    is_second = jnp.max(jnp.where(same & earlier & (subs < 72), 1, 0), axis=1, keepdims=True)
    is_second = jnp.broadcast_to(is_second, (128, 128))
    second_row = is_second.T
    rank = jnp.sum(jnp.where(earlier, second_row, 0), axis=1, keepdims=True)
    rank = jnp.broadcast_to(rank, (128, 128))
    rank_row = rank.T
    mine = owners == subs
    first = jnp.min(jnp.where(mine, lanes, 71), axis=1, keepdims=True)
    entry = jnp.sum(jnp.where(mine, second_row * rank_row, 0), axis=1, keepdims=True)
    numbers = jnp.sum(jnp.where(rank == lanes, is_second * subs, 0), axis=0, keepdims=True)
    entry = jnp.minimum(entry, SPARE - 1)
    table_v[...] = jnp.where(subs == 64, numbers, jnp.where(lanes == 0, first, entry))
    table_copy = pltpu.make_async_copy(table_v, table_s, t_sem)
    table_copy.start()
    table_copy.wait()

    for n in range(3):
        own_piece(n, 0).wait_recv()
        forward_piece(n, 0).start()
        own_piece(5 - n, 1).wait_recv()
        forward_piece(5 - n, 1).start()
    for n in range(3, 6):
        own_piece(n, 0).wait_recv()
        own_piece(5 - n, 1).wait_recv()
    core_shard(3, 2).start()
    core_shard(1, 3).start()
    for n in range(3):
        forward_piece(n, 0).wait_recv()
        core_piece(n).start()
        forward_piece(5 - n, 1).wait_recv()
        core_piece(5 - n).start()
    cot_copy.wait_recv()
    core_shard(0, 1).wait_recv()
    core_shard(3, 2).wait_recv()
    core_shard(1, 3).wait_recv()
    for p in range(PIECES):
        core_piece(p).wait_recv()

    def product_of(block):
        band = lax.rem(lax.div(block, 6) - 3 * x + 12, 12)
        column = lax.rem(block, 6)
        total = jnp.dot(at[0, band], cot2[0, column], preferred_element_type=jnp.float32)
        total += jnp.dot(at[1, band], cot2[1, column], preferred_element_type=jnp.float32)
        return total * token_scale

    @pl.loop(0, SPARE // 2)
    def _(s):
        spill[...] = product_of(table_s[64, 2 * s + c]).reshape(NQ, 8, BLK)

        @pl.loop(0, NQ)
        def _(q):
            dz = lax.rem(lax.div(q, NY) - z + NZ, NZ)
            dy = lax.rem(lax.rem(q, NY) - y + NY, NY)
            part[dz, dy, pl.ds(pl.multiple_of(BLK + 8 * s, 8), 8), :] = spill[q]

    def produce(dz):
        @pl.loop(0, NY)
        def _(dy):
            q = lax.rem(z + dz, NZ) * NY + lax.rem(y + dy, NY)
            part[dz, dy, pl.ds(0, BLK), :] = product_of(table_s[2 * q + c, 0])

    def rows_of(dz, dy, start):
        def read(g):
            return part[dz, dy, pl.ds(start + 16 * g, 16), :]

        return read

    def both(first_read, second_read, low=0, high=1000):
        def read(g):
            if low <= g < high:
                return first_read(g) + second_read(g - low)
            return first_read(g)

        return read

    def hop(src, dst, sems, index, target):
        return remote(src.at[index], dst.at[index], sems.at[(0,) + index], sems.at[(1,) + index], target)

    def y_target(d):
        return device(dy=1 - 2 * d)

    def z_target(d):
        return device(dz=1 - 2 * d)

    GA, GB = RA // 16, RB // 16

    def dirs(body):
        for d in range(2):
            body(d)

    def a_y2(dz):
        def body(d):
            encode(rows_of(dz, 2, d * (RA // 2)), GA // 2, ya2_s.at[dz, d])
            hop(ya2_s, ya2_r, ya2_sem, (dz, d), y_target(d)).start()

        dirs(body)

    def a_y1(dz):
        def body(d):
            hop(ya2_s, ya2_r, ya2_sem, (dz, d), y_target(d)).wait_recv()
            arrived = decoder(ya2_r.at[dz, d], GA // 2)
            low = d * (GA // 2)
            encode(both(rows_of(dz, 1 + 2 * d, 0), arrived, low, low + GA // 2), GA, ya1_s.at[dz, d])
            hop(ya1_s, ya1_r, ya1_sem, (dz, d), y_target(d)).start()

        dirs(body)

    def a_yf(dz):
        for d in range(2):
            hop(ya1_s, ya1_r, ya1_sem, (dz, d), y_target(d)).wait_recv()
        left, right = decoder(ya1_r.at[dz, 0], GA), decoder(ya1_r.at[dz, 1], GA)
        for g in range(GA):
            part[dz, 0, pl.ds(16 * g, 16), :] += left(g) + right(g)

    def a_z(k):
        def body(d):
            if k == 4:
                encode(rows_of(4, 0, d * (RA // 2)), GA // 2, za4_s.at[d])
                hop(za4_s, za4_r, za4_sem, (d,), z_target(d)).start()
                return
            dz = k if d == 0 else 8 - k
            if k == 3:
                hop(za4_s, za4_r, za4_sem, (d,), z_target(d)).wait_recv()
                low = d * (GA // 2)
                read = both(rows_of(dz, 0, 0), decoder(za4_r.at[d], GA // 2), low, low + GA // 2)
            else:
                hop(za_s, za_r, za_sem, (k, d), z_target(d)).wait_recv()
                read = both(rows_of(dz, 0, 0), decoder(za_r.at[k, d], GA))
            encode(read, GA, za_s.at[k - 1, d])
            hop(za_s, za_r, za_sem, (k - 1, d), z_target(d)).start()

        dirs(body)

    def b_z(k):
        @pl.loop(0, NY)
        def _(n):
            dy = lax.rem(n + 2, NY)

            def body(d):
                if k == 4:
                    encode(rows_of(4, dy, RA + d * (RB // 2)), GB // 2, zb4_s.at[dy, d])
                    hop(zb4_s, zb4_r, zb4_sem, (dy, d), z_target(d)).start()
                    return
                dz = k if d == 0 else 8 - k
                if k == 3:
                    hop(zb4_s, zb4_r, zb4_sem, (dy, d), z_target(d)).wait_recv()
                    low = d * (GB // 2)
                    read = both(rows_of(dz, dy, RA), decoder(zb4_r.at[dy, d], GB // 2), low, low + GB // 2)
                else:
                    hop(zb_s, zb_r, zb_sem, (k, dy, d), z_target(d)).wait_recv()
                    read = both(rows_of(dz, dy, RA), decoder(zb_r.at[k, dy, d], GB))
                encode(read, GB, zb_s.at[k - 1, dy, d])
                hop(zb_s, zb_r, zb_sem, (k - 1, dy, d), z_target(d)).start()

            dirs(body)

    def b_zf(dy):
        for d in range(2):
            hop(zb_s, zb_r, zb_sem, (0, dy, d), z_target(d)).wait_recv()
        left, right = decoder(zb_r.at[0, dy, 0], GB), decoder(zb_r.at[0, dy, 1], GB)
        for g in range(GB):
            part[0, dy, pl.ds(RA + 16 * g, 16), :] += left(g) + right(g)

    def b_y2():
        def body(d):
            encode(rows_of(0, 2, RA + d * (RB // 2)), GB // 2, yb2_s.at[d])
            hop(yb2_s, yb2_r, yb2_sem, (d,), y_target(d)).start()

        dirs(body)

    def b_y1():
        def body(d):
            hop(yb2_s, yb2_r, yb2_sem, (d,), y_target(d)).wait_recv()
            arrived = decoder(yb2_r.at[d], GB // 2)
            low = d * (GB // 2)
            encode(both(rows_of(0, 1 + 2 * d, RA), arrived, low, low + GB // 2), GB, yb1_s.at[d])
            hop(yb1_s, yb1_r, yb1_sem, (d,), y_target(d)).start()

        dirs(body)

    produce(4)
    b_z(4)
    a_y2(4)
    produce(3)
    produce(5)
    a_y2(3)
    a_y2(5)
    b_z(3)
    a_y1(4)
    produce(2)
    produce(6)
    a_y2(2)
    a_y2(6)
    a_y1(3)
    a_y1(5)
    b_z(2)
    a_yf(4)
    a_z(4)
    produce(1)
    produce(7)
    a_y2(1)
    a_y2(7)
    a_y1(2)
    a_y1(6)
    a_yf(3)
    a_yf(5)
    a_z(3)
    b_z(1)
    produce(0)
    a_y2(0)
    a_y1(1)
    a_y1(7)
    a_yf(2)
    a_yf(6)
    a_z(2)
    b_zf(2)
    b_y2()
    a_y1(0)
    a_yf(1)
    a_yf(7)
    a_z(1)
    b_zf(1)
    b_zf(3)
    b_y1()
    b_zf(0)
    a_yf(0)

    for d in range(2):
        hop(yb1_s, yb1_r, yb1_sem, (d,), y_target(d)).wait_recv()
    left, right = decoder(yb1_r.at[0], GB), decoder(yb1_r.at[1], GB)
    for g in range(GB):
        rows = part[0, 0, pl.ds(RA + 16 * g, 16), :] + left(g) + right(g)
        if g < 6:
            primary_ref[pl.ds(RA + 16 * g, 16), :] = rows
        else:
            sec[c, pl.ds(2 * (g - 6), 2)] = rows.reshape(2, 8, BLK)
    sec_copy = remote(sec.at[c], sec.at[c], s_sem.at[0], s_sem.at[1], other)
    sec_copy.start()

    for d in range(2):
        hop(za_s, za_r, za_sem, (0, d), z_target(d)).wait_recv()
    left, right = decoder(za_r.at[0, 0], GA), decoder(za_r.at[0, 1], GA)
    for g in range(GA):
        primary_ref[pl.ds(16 * g, 16), :] = part[0, 0, pl.ds(16 * g, 16), :] + left(g) + right(g)

    sec_copy.wait_recv()

    @pl.loop(0, NQ)
    def _(q):
        place_of = table_s[2 * q + c, 1]
        sec_out[q] = sec[lax.rem(place_of, 2), lax.div(place_of, 2)]

    @pl.loop(1, NQ)
    def _(r):
        q = lax.rem(me_q + r, NQ)
        remote(sec_out.at[q], sec_in.at[me_q], s_sem.at[2], s_sem.at[3], (q * 2 + c, x)).start()

    whole = remote(sec_out.at[pl.ds(0, NQ - 1)], sec_in.at[pl.ds(0, NQ - 1)], s_sem.at[2], s_sem.at[3], other)
    whole.wait_recv()
    second_ref[...] = sec_in[...]
    second_ref[me_q] = sec_out[me_q]

    whole.wait_send()
    sec_copy.wait_send()
    cot_copy.wait_send()
    core_shard(0, 1).wait_send()
    core_shard(3, 2).wait_send()
    core_shard(1, 3).wait_send()
    for p in range(PIECES):
        core_piece(p).wait_send()
        own_piece(p, 0).wait_send()
        own_piece(p, 1).wait_send()
        forward_piece(p, 0 if p < 3 else 1).wait_send()
    for d in range(2):
        for dz in range(NZ):
            hop(ya2_s, ya2_r, ya2_sem, (dz, d), y_target(d)).wait_send()
            hop(ya1_s, ya1_r, ya1_sem, (dz, d), y_target(d)).wait_send()
        hop(za4_s, za4_r, za4_sem, (d,), z_target(d)).wait_send()
        hop(yb2_s, yb2_r, yb2_sem, (d,), y_target(d)).wait_send()
        hop(yb1_s, yb1_r, yb1_sem, (d,), y_target(d)).wait_send()
        for k in range(3):
            hop(za_s, za_r, za_sem, (k, d), z_target(d)).wait_send()
            for dy in range(NY):
                hop(zb_s, zb_r, zb_sem, (k, dy, d), z_target(d)).wait_send()
        for dy in range(NY):
            hop(zb4_s, zb4_r, zb4_sem, (dy, d), z_target(d)).wait_send()


def owner_gradients(activations, cotangent, block_owner, token_scale):
    owner_row = jnp.pad(block_owner, (0, 56), constant_values=-1).reshape(1, 128)
    i16, f32, i32, bf16 = jnp.int16, jnp.float32, jnp.int32, jnp.bfloat16
    vmem, dma = pltpu.VMEM, pltpu.SemaphoreType.DMA

    def pair(shape):
        return [vmem(shape, i16), vmem(shape, i16)]

    ha, hb = RA // 2 + 16, RB // 2 + 16
    fa, fb = RA + 16, RB + 16
    return pl.pallas_call(
        functools.partial(gradient_kernel, token_scale),
        out_shape=(
            jax.ShapeDtypeStruct((BLK, BLK), f32),
            jax.ShapeDtypeStruct((NQ, 8, BLK), f32),
        ),
        in_specs=[pl.BlockSpec(memory_space=pltpu.VMEM)] * 3,
        out_specs=[pl.BlockSpec(memory_space=pltpu.VMEM)] * 2,
        scratch_shapes=[
            vmem((128, 128), i32),
            pltpu.SMEM((128, 128), i32),
            vmem((2, 3 * NX, BLK, 512), bf16),
            vmem((2, 6, 512, BLK), bf16),
            vmem((NZ, NY, RA + RB, BLK), f32),
            vmem((NQ, 8, BLK), f32),
        ]
        + pair((NZ, 2, ha, BLK))
        + pair((NZ, 2, fa, BLK))
        + pair((2, ha, BLK))
        + pair((3, 2, fa, BLK))
        + pair((NY, 2, hb, BLK))
        + pair((3, NY, 2, fb, BLK))
        + pair((2, hb, BLK))
        + pair((2, fb, BLK))
        + [
            vmem((2, SPARE // 2, 8, BLK), f32),
            vmem((NQ, 8, BLK), f32),
            vmem((NQ, 8, BLK), f32),
            dma((2, PIECES)),
            dma((2, PIECES)),
            dma((PIECES,)),
            dma((PIECES,)),
            dma((10,)),
            dma((10,)),
            dma((2, NZ, 2)),
            dma((2, NZ, 2)),
            dma((2, 2)),
            dma((2, 3, 2)),
            dma((2, NY, 2)),
            dma((2, 3, NY, 2)),
            dma((2, 2)),
            dma((2, 2)),
            dma,
            dma((4,)),
        ],
        compiler_params=pltpu.CompilerParams(
            collective_id=0, has_side_effects=True, vmem_limit_bytes=48 * 1024 * 1024
        ),
    )(owner_row, activations, cotangent)


def product(left_side, right_side):
    return jnp.dot(left_side, right_side, precision=HIGHEST, preferred_element_type=jnp.float32)


def orthogonalize(matrix):
    current = matrix / jnp.sqrt(jnp.sum(matrix * matrix) + EPS)
    identity = jnp.eye(matrix.shape[0], dtype=jnp.float32)
    for _ in range(NSTEPS):
        current = product(current, 1.5 * identity - 0.5 * product(current.T, current))
    return current


def refresh(gradient, left_old, right_old, left_prev, right_prev):
    order_size = gradient.shape[0]
    left_new = BETA * left_old + (1.0 - BETA) / order_size * product(gradient, gradient.T)
    right_new = BETA * right_old + (1.0 - BETA) / order_size * product(gradient.T, gradient)
    left_power = product(left_new, left_prev)
    right_power = product(right_new, right_prev)
    left_fresh = orthogonalize(left_power)
    right_fresh = orthogonalize(right_power)
    left_scale = (jnp.mean(left_power * left_power, axis=0) + EPS) ** (-0.125)
    right_scale = (jnp.mean(right_power * right_power, axis=0) + EPS) ** (-0.125)
    rotated = product(product(left_fresh.T, gradient), right_fresh)
    rotated = rotated * left_scale[:, None] * right_scale[None, :]
    block_update = product(product(left_fresh, rotated), right_fresh.T).astype(jnp.bfloat16)
    return (block_update, left_new, right_new, left_fresh, right_fresh)


def slot_numbers(block_owner, capacity):
    positions = jnp.arange(block_owner.shape[0], dtype=jnp.int32)
    same_owner = block_owner[:, None] == block_owner[None, :]
    earlier = positions[None, :] < positions[:, None]
    slot_rank = jnp.sum(jnp.where(same_owner & earlier, 1, 0), axis=1).astype(jnp.int32)
    return block_owner * capacity + slot_rank


def on_device(
    activations, cotangent, block_owner, left_factor, right_factor, left_basis, right_basis
):
    dp_count = lax.axis_size("dp")
    token_scale = 1.0 / math.sqrt(activations.shape[0] * dp_count)
    slot_ids = slot_numbers(block_owner, 2)
    primary, second = owner_gradients(activations, cotangent, block_owner, token_scale)
    own_index = lax.axis_index("dp")
    held = jnp.sum(jnp.where(block_owner == own_index, 1, 0))
    live_here = jnp.stack([held > 0, held > 1])
    owned_blocks = jnp.stack([primary, second.reshape(BLK, BLK)])

    def handle_slot(unused_carry, slot_entry):
        is_live = slot_entry[0]
        operands = slot_entry[1:]

        def refresh_slot(values):
            return refresh(*values)

        def skip_slot(values):
            return (
                jnp.zeros(values[0].shape, jnp.bfloat16),
                values[1],
                values[2],
                values[3],
                values[4],
            )

        return (unused_carry, lax.cond(is_live, refresh_slot, skip_slot, operands))

    _, results = lax.scan(
        handle_slot,
        jnp.zeros((), jnp.int32),
        (live_here, owned_blocks, left_factor, right_factor, left_basis, right_basis),
    )
    updates, left_next, right_next, left_basis_next, right_basis_next = results
    outgoing = jnp.swapaxes(updates, 0, 1)
    returned = lax.all_to_all(outgoing, "dp", split_axis=0, concat_axis=1, tiled=True)
    own_rows = jnp.take(returned, slot_ids, axis=1)
    update = own_rows.reshape(own_rows.shape[0], 12, 1536)
    return (update, left_next, right_next, left_basis_next, right_basis_next)


def solution(mesh):
    placed = (
        P("dp", "mp"),
        P("dp", "mp"),
        P(),
        P("dp", "mp", None),
        P("dp", "mp", None),
        P("dp", "mp", None),
        P("dp", "mp", None),
    )
    return jax.shard_map(
        on_device,
        mesh=mesh,
        in_specs=placed,
        out_specs=(
            P("dp", None, "mp"),
            P("dp", "mp", None),
            P("dp", "mp", None),
            P("dp", "mp", None),
            P("dp", "mp", None),
        ),
        check_vma=False,
    )
```

time: 432 us -> 187 us (0.43)
  waiting for transfers between devices: 292 us -> 12.7 us
  Pallas kernels: 0 us -> 92.7 us
  local copies, waits for them, and re-layouts: 42.4 us -> 18 us
  between operations: 14.3 us -> 2.1 us
  matrix products: 34.7 us -> 23.8 us
  starting transfers between devices: 42.4 us -> 32.7 us
    reduce_scatter x1 -> x0, waiting for transfers between devices: 216 us -> none  [on_device(): lax.psum_scatter(partial_value * token_scale, 'dp', scatter_dimension=0,...]
    pallas_call x0 -> x1, Pallas kernels: none -> 92.7 us  [owner_gradients(): pl.pallas_call(functools.partial(gradient_kernel, token_scale), out_shape...]
    all_gather x1 -> x0, waiting for transfers between devices: 46 us -> none  [on_device(): gathered = lax.all_gather(activations, 'mp', axis=1, tiled=True)]
    mul x1 -> x0, local copies, waits for them, and re-layouts: 22.6 us -> none  [on_device(): partial_value * token_scale]
    all_to_all x1 -> x0, waiting for transfers between devices: 17.6 us -> none  [on_device(): lax.all_to_all(outgoing_rows, 'dp', split_axis=1, concat_axis=0, tiled=True)]
    all_to_all x1 -> x0, starting transfers between devices: 11.8 us -> none  [on_device(): lax.all_to_all(outgoing_rows, 'dp', split_axis=1, concat_axis=0, tiled=True)]
    dot_general x1 -> x0, matrix products: 11 us -> none  [on_device(): jnp.einsum('tir,tc->ric', banded, cotangent, preferred_element_type=jnp.f...]
  transfers between devices with their start and end apart: 4 -> 1, of which waited for: 4 -> 1; matrix products, arithmetic and copies ran while one was open for 0% -> 0% of each run, Pallas kernels for 0% -> 0%
where the time goes in v1:
time: 187 us
  Pallas kernels  92.7 us (50%)
  starting transfers between devices  32.7 us (17%)
  matrix products  23.8 us (13%)
  local copies, waits for them, and re-layouts  18 us (10%)
  waiting for transfers between devices  12.7 us (7%)
  loops' own time  3.14 us (2%)
  between operations  2.1 us (1%)
    pallas_call x1, Pallas kernels, owner_gradients(): pl.pallas_call(functools.partial(gradient_kernel, token_scale), out_shape...  92.7 us
    all_to_all x1, starting transfers between devices, on_device(): lax.all_to_all(outgoing, 'dp', split_axis=0, concat_axis=1, tiled=True)  32.7 us
    dot_general x32, matrix products, product(): jnp.dot(left_side, right_side, precision=HIGHEST, preferred_element_type=...  23.8 us
    all_to_all x1, waiting for transfers between devices, on_device(): lax.all_to_all(outgoing, 'dp', split_axis=0, concat_axis=1, tiled=True)  12.7 us
    dynamic_update_slice x6, local copies, waits for them, and re-layouts, on_device(): lax.scan(handle_slot, jnp.zeros((), jnp.int32), (live_here, owned_blocks,...  6.7 us
  transfers between devices with their start and end apart: 1, of which 1 were waited for; matrix products, arithmetic and copies ran while one was open for 0% of the time, Pallas kernels for 0%

profile of v1, /device:TPU:1, one launch (start us, length us, event | category | flops | bytes accessed | tf_op | source)
XLA Modules:
  0.0 186.7 jit_solution(15238082716636135922)
XLA Ops:
  0.7 0.7 pad_bitcast_fusion.owner_ref
  1.3 1.4 fusion.17
  4.1 1.4 copy-done
  5.5 1.1 copy-done.1
  6.6 92.7 %shard_map.110 = (f32[256,256]{1,0:T(8,128)S(1)}, f32[32,8,256]{2,1,0:T(8,128)S(1)}) custom-call(s32[1,128]{1,0:T(1,128)S(1)} %pad_bitcast_fusion.owner_ref, bf16[512,768]{1,0:T(8,128)(2,1)S(1)} %copy-done.1, bf16[512,1536]{1,0:T(8,128)(2,1)S(1)} %copy-done), custom_call_target="tpu_custom_call" | custom-call | tf_op jit(solution)/shard_map/pallas_call | solution.py:472
  99.4 37.8 %while.18 = (s32[]{:T(128)}, bf16[2,256,256]{2,1,0:T(8,128)(2,1)}, f32[2,256,256]{2,1,0:T(8,128)}, f32[2,256,256]{2,1,0:T(8,128)}, f32[2,256,256]{2,1,0:T(8,128)...) while((s32[]{:T(128)}, bf16[2,256,256]{2,1,0:T(8,128)(2,1)}, ...), condition=%wide.region_9.10_spmd, body=%wide.region_2.9_spmd.sunk | while | flops 6446842368 | bytes 26355548 | solution.py:589
  99.6 0.7 dynamic-slice_bitcast_fusion.10
  100.3 0.7 dynamic-slice_bitcast_fusion.11
  101.0 0.6 dynamic_slice.48
  102.3 25.4 %conditional.2 = (f32[256,256]{1,0:T(8,128)S(1)}, f32[256,256]{1,0:T(8,128)S(1)}, f32[256,256]{1,0:T(8,128)}, f32[256,256]{1,0:T(8,128)}, bf16[1,256,256]{2,1,0:T(8,128)(2,1)S(1)}) conditional(s32[]{:T(128)} %bitcast.109, (f32[256,256]{1,0:T(8,128)S(1)}, f32[256,256]{1,0:T(8,128)S(1)}, f32[256,256]{1,0:T(8,128)}, f32[256,256]{1,0:T(8,128)}) %tuple.51, ...), branch_computations={%region_3.3_spmd, %region_4.8_spmd} | conditional | flops 6446842368 | bytes 21897332 | solution.py:587
  102.3 0.7 fusion.1
  103.0 2.0 %multiply_reduce_fusion = (f32[256]{0:T(256)S(1)}, f32[]{:T(128)}, f32[256,256]{1,0:T(8,128)S(1)}) fusion(f32[256,256]{1,0:T(8,128)S(1)} %fusion.1, f32[256,256]{1,0:T(8,128)} %get-tuple-element.93), kind=kOutput, calls=%fused_computation.38 | convolution fusion | flops 201522944 | bytes 787460 | tf_op jit(solution)/shard_map/while/body/eval_jaxpr/cond/branch_1_fun/dot_general | solution.py:524
  111.2 1.1 fusion.27
  112.8 2.0 %multiply_reduce_fusion.2 = (f32[256]{0:T(256)S(1)}, f32[]{:T(128)}, f32[256,256]{1,0:T(8,128)S(1)}) fusion(f32[256,256]{1,0:T(8,128)S(1)} %fusion.2, f32[256,256]{1,0:T(8,128)} %get-tuple-element.92), kind=kOutput, calls=%fused_computation.40 | convolution fusion | flops 201522944 | bytes 787460 | tf_op jit(solution)/shard_map/while/body/eval_jaxpr/cond/branch_1_fun/dot_general | solution.py:524
  121.0 1.1 fusion.22
  122.1 1.5 fusion.4
  123.6 1.3 fusion
  125.0 1.3 fusion.28
  126.3 1.4 fusion.3
  127.7 1.9 bitcast_dynamic-update-slice_fusion.7
  129.5 0.8 bitcast_dynamic-update-slice_fusion.6
  130.4 0.7 constant_dynamic-update-slice_fusion.2
  131.0 0.7 dynamic-slice_bitcast_fusion.10
  131.7 0.7 dynamic-slice_bitcast_fusion.11
  133.8 1.9 bitcast_dynamic-update-slice_fusion.7
  135.7 0.8 bitcast_dynamic-update-slice_fusion.6
  136.5 0.7 constant_dynamic-update-slice_fusion.2
  137.1 1.9 %copy.25 = bf16[2,256,256]{2,0,1:T(2,128)(2,1)} copy(bf16[2,256,256]{2,1,0:T(8,128)(2,1)} %get-tuple-element.126) | data formatting | bytes 524288 | tf_op jit(solution)/shard_map/while | solution.py:589
  139.1 32.7 %all-to-all-start = ((bf16[256,2,256]{2,1,0:T(2,128)(2,1)}), bf16[256,2,256]{2,1,0:T(2,128)(2,1)S(1)}, u32[]{:S(2)}, u32[]{:S(2)}) async-start(bf16[256,2,256]{2,1,0:T(2,128)(2,1)} %bitcast.95), calls=%async_computation | async-start | bytes 524288 | tf_op jit(solution)/shard_map/all_to_all | solution.py:596
  172.2 12.7 %all-to-all-done = bf16[256,2,256]{2,1,0:T(2,128)(2,1)S(1)} async-done(((bf16[256,2,256]{2,1,0:T(2,128)(2,1)}), bf16[256,2,256]{2,1,0:T(2,128)(2,1)S(1)}, u32[]{:S(2)}, u32[]{:S(2)}) %all-to-all-start) | async-done | bytes 262176 | tf_op jit(solution)/shard_map/all_to_all | solution.py:596
  185.0 0.7 gather_fusion
  186.0 0.8 copy.22
  (61 shorter events, 13.1 us)
Async XLA Ops:
  4.1 1.4 copy-start
  5.5 1.1 copy-start.1
  6.6 92.7 %copy-start.2 = (f32[2,256,256]{2,1,0:T(8,128)S(1)}, f32[2,256,256]{2,1,0:T(8,128)}, u32[]{:S(2)}) copy-start(f32[2,256,256]{2,1,0:T(8,128)} %param.14) | copy-start | bytes 1572868
  6.6 92.7 %copy-start.3 = (f32[2,256,256]{2,1,0:T(8,128)S(1)}, f32[2,256,256]{2,1,0:T(8,128)}, u32[]{:S(2)}) copy-start(f32[2,256,256]{2,1,0:T(8,128)} %param.15) | copy-start | bytes 1572868
  6.6 92.7 %copy-start.4 = (f32[2,256,256]{2,1,0:T(8,128)S(1)}, f32[2,256,256]{2,1,0:T(8,128)}, u32[]{:S(2)}) copy-start(f32[2,256,256]{2,1,0:T(8,128)} %param.16) | copy-start | bytes 1572868
  6.6 92.7 %copy-start.5 = (f32[2,256,256]{2,1,0:T(8,128)S(1)}, f32[2,256,256]{2,1,0:T(8,128)}, u32[]{:S(2)}) copy-start(f32[2,256,256]{2,1,0:T(8,128)} %param.17) | copy-start | bytes 1572868
  99.3 72.4 %copy-start.6 = (s32[72]{0:T(128)S(1)}, s32[72]{0:T(128)}, u32[]{:S(2)}) copy-start(s32[72]{0:T(128)} %param.13) | copy-start | bytes 868
  139.1 45.9 %all-to-all-start = ((bf16[256,2,256]{2,1,0:T(2,128)(2,1)}), bf16[256,2,256]{2,1,0:T(2,128)(2,1)S(1)}, u32[]{:S(2)}, u32[]{:S(2)}) async-start(bf16[256,2,256]{2,1,0:T(2,128)(2,1)} %bitcast.95), calls=%async_computation | async-start | bytes 524288 | tf_op jit(solution)/shard_map/all_to_all | solution.py:596

commit v2 on v1

--- a/solution.py
+++ b/solution.py
@@ -11,7 +11,6 @@
 NSTEPS = 6
 BETA = 0.9
 EPS = 1e-06
-HIGHEST = lax.Precision.HIGHEST
 MESH = pl.DeviceIdType.MESH
 NX, NY, NZ, NQ = 4, 4, 8, 32
 BLK = 256
@@ -66,13 +65,76 @@
     return read
 
 
+def split(value):
+    high = value.astype(jnp.bfloat16)
+    return high, (value - high.astype(jnp.float32)).astype(jnp.bfloat16)
+
+
+def turned(parts):
+    return parts[0].T, parts[1].T
+
+
+def times(left_parts, right_parts):
+    def dot(a, b):
+        return jnp.dot(a, b, preferred_element_type=jnp.float32)
+
+    low = dot(left_parts[1], right_parts[0]) + dot(left_parts[0], right_parts[1])
+    return dot(left_parts[0], right_parts[0]) + low
+
+
+def refresh(gradient, held, fresh, k, live):
+    def keep(n, value):
+        fresh[n, k] = value if live is None else jnp.where(live, value, held[n, k])
+
+    g = split(gradient)
+    gt = turned(g)
+    share = (1.0 - BETA) / BLK
+    factors = [BETA * held[0, k] + share * times(g, gt), BETA * held[1, k] + share * times(gt, g)]
+    powers, scales = [], []
+    for n in range(2):
+        keep(n, factors[n])
+        power = times(split(factors[n]), split(held[2 + n, k]))
+        square = jnp.sum(power * power, axis=0, keepdims=True)
+        scales.append(jnp.exp(-0.125 * jnp.log(square * (1.0 / BLK) + EPS)))
+        powers.append(power / jnp.sqrt(jnp.sum(square, axis=1, keepdims=True) + EPS))
+
+    def step(_, values):
+        parts = [split(v) for v in values]
+        grams = [times(turned(p), p) for p in parts]
+        moves = [times(p, split(gram)) for p, gram in zip(parts, grams)]
+        return tuple(1.5 * v - 0.5 * m for v, m in zip(values, moves))
+
+    bases = lax.fori_loop(0, NSTEPS, step, tuple(powers))
+    weights = []
+    for n in range(2):
+        keep(2 + n, bases[n])
+        weights.append(times(split(bases[n] * scales[n]), turned(split(bases[n]))))
+    inner = times(g, split(weights[1]))
+    return times(split(weights[0]), split(inner))
+
+
 def gradient_kernel(
     token_scale,
     owner_ref,
+    act_hbm,
+    cot_hbm,
+    left_hbm,
+    right_hbm,
+    left_basis_hbm,
+    right_basis_hbm,
+    update_ref,
+    left_out,
+    right_out,
+    left_basis_out,
+    right_basis_out,
+    owner_v,
     act_ref,
-    cot_ref,
-    primary_ref,
-    second_ref,
+    held,
+    fresh,
+    grad,
+    u_send,
+    ret,
+    stage,
     table_v,
     table_s,
     at,
@@ -114,11 +176,39 @@
     yb1_sem,
     t_sem,
     s_sem,
+    in_sem,
+    held_sem,
+    out_sem,
+    u_sem,
+    r_sem,
 ):
     x, y, z, c = place()
     me_q = z * NY + y
     other = device(dc=1)
 
+    def act_in(n):
+        columns = pl.ds(n * 384, 384)
+        return pltpu.make_async_copy(act_hbm.at[:, columns], act_ref.at[:, columns], in_sem.at[6 + n])
+
+    def cot_in(j):
+        return pltpu.make_async_copy(cot_hbm.at[:, pl.ds(j * BLK, BLK)], cot2.at[0, j], in_sem.at[j])
+
+    factors = (left_hbm, right_hbm, left_basis_hbm, right_basis_hbm)
+    results = (left_out, right_out, left_basis_out, right_basis_out)
+
+    def held_in(n):
+        return pltpu.make_async_copy(factors[n], held.at[n], held_sem.at[n])
+
+    def fresh_out(n, k):
+        return pltpu.make_async_copy(fresh.at[n, k], results[n].at[k], out_sem.at[n, k])
+
+    act_in(0).start()
+    act_in(1).start()
+    for j in range(6):
+        cot_in(j).start()
+    for n in range(4):
+        held_in(n).start()
+
     barrier = pltpu.get_barrier_semaphore()
     for target in (device(dx=1), device(dx=3), other):
         pl.semaphore_signal(barrier, inc=1, device_id=target, device_id_type=MESH)
@@ -135,6 +225,8 @@
         at[0, p // 2, pl.ds((p % 2) * PROWS, PROWS), :] = act_ref[:, pl.ds(p * PROWS, PROWS)].T
 
     order = (0, 5, 1, 4, 2, 3)
+    act_in(0).wait()
+    act_in(1).wait()
     turn(order[0])
     pl.semaphore_wait(barrier, NQ + 2)
 
@@ -162,15 +254,18 @@
         own_piece(p, 1).start()
     core_shard(0, 1).start()
     for j in range(6):
-        cot2[0, j] = cot_ref[:, pl.ds(j * BLK, BLK)]
+        cot_in(j).wait()
     cot_copy = remote(cot2.at[0], cot2.at[1], c_send.at[0], c_recv.at[0], other)
     cot_copy.start()
 
-    owners = owner_ref[...]
+    owner_v[...] = jnp.full((1, 128), -1, jnp.int32)
+    owner_v[:, pl.ds(0, 72)] = owner_ref[...]
+    owners = owner_v[...]
     lanes = lax.broadcasted_iota(jnp.int32, (128, 128), 1)
     subs = lax.broadcasted_iota(jnp.int32, (128, 128), 0)
     earlier = lanes < subs
-    same = jnp.broadcast_to(owners, (128, 128)).T == owners
+    owner_column = jnp.broadcast_to(owners, (128, 128)).T
+    same = owner_column == owners
     is_second = jnp.max(jnp.where(same & earlier & (subs < 72), 1, 0), axis=1, keepdims=True)
     is_second = jnp.broadcast_to(is_second, (128, 128))
     second_row = is_second.T
@@ -182,7 +277,11 @@
     entry = jnp.sum(jnp.where(mine, second_row * rank_row, 0), axis=1, keepdims=True)
     numbers = jnp.sum(jnp.where(rank == lanes, is_second * subs, 0), axis=0, keepdims=True)
     entry = jnp.minimum(entry, SPARE - 1)
-    table_v[...] = jnp.where(subs == 64, numbers, jnp.where(lanes == 0, first, entry))
+    count = jnp.sum(jnp.where(mine, 1, 0), axis=1, keepdims=True)
+    slots = jnp.where(subs < 72, 2 * owner_column + is_second, 0)
+    columns = jnp.where(lanes == 0, first, jnp.where(lanes == 1, entry, jnp.where(lanes == 2, slots, count)))
+    table_v[0:128, :] = columns
+    table_v[128:136, :] = jnp.broadcast_to(numbers, (8, 128))
     table_copy = pltpu.make_async_copy(table_v, table_s, t_sem)
     table_copy.start()
     table_copy.wait()
@@ -218,7 +317,7 @@
 
     @pl.loop(0, SPARE // 2)
     def _(s):
-        spill[...] = product_of(table_s[64, 2 * s + c]).reshape(NQ, 8, BLK)
+        spill[...] = product_of(table_s[128, 2 * s + c]).reshape(NQ, 8, BLK)
 
         @pl.loop(0, NQ)
         def _(q):
@@ -404,7 +503,7 @@
     for g in range(GB):
         rows = part[0, 0, pl.ds(RA + 16 * g, 16), :] + left(g) + right(g)
         if g < 6:
-            primary_ref[pl.ds(RA + 16 * g, 16), :] = rows
+            grad[0, pl.ds(RA + 16 * g, 16), :] = rows
         else:
             sec[c, pl.ds(2 * (g - 6), 2)] = rows.reshape(2, 8, BLK)
     sec_copy = remote(sec.at[c], sec.at[c], s_sem.at[0], s_sem.at[1], other)
@@ -414,7 +513,7 @@
         hop(za_s, za_r, za_sem, (0, d), z_target(d)).wait_recv()
     left, right = decoder(za_r.at[0, 0], GA), decoder(za_r.at[0, 1], GA)
     for g in range(GA):
-        primary_ref[pl.ds(16 * g, 16), :] = part[0, 0, pl.ds(16 * g, 16), :] + left(g) + right(g)
+        grad[0, pl.ds(16 * g, 16), :] = part[0, 0, pl.ds(16 * g, 16), :] + left(g) + right(g)
 
     sec_copy.wait_recv()
 
@@ -429,9 +528,57 @@
         remote(sec_out.at[q], sec_in.at[me_q], s_sem.at[2], s_sem.at[3], (q * 2 + c, x)).start()
 
     whole = remote(sec_out.at[pl.ds(0, NQ - 1)], sec_in.at[pl.ds(0, NQ - 1)], s_sem.at[2], s_sem.at[3], other)
+    for n in range(4):
+        held_in(n).wait()
+
+    def u_whole(k):
+        part_of = pl.ds(0, NQ - 1)
+        return remote(u_send.at[k, part_of], ret.at[k, c, part_of], u_sem.at[0, k], u_sem.at[1, k], other)
+
+    def u_core(k):
+        return remote(ret.at[k, c], ret.at[k, c], r_sem.at[0, k], r_sem.at[1, k], other)
+
+    def finish(k):
+        update = refresh(grad[k], held, fresh, k, None if k == 0 else table_s[me_q * 2 + c, 3] > 1)
+        for n in range(4):
+            fresh_out(n, k).start()
+        rows = update.reshape(NQ, 8, BLK)
+        halves = jnp.concatenate([rows[:, :, : BLK // 2], rows[:, :, BLK // 2 :]], axis=1)
+        u_send[k] = halves.astype(jnp.bfloat16)
+
+        @pl.loop(1, NQ)
+        def _(r):
+            q = lax.rem(me_q + r, NQ)
+            remote(u_send.at[k, q], ret.at[k, c, me_q], u_sem.at[0, k], u_sem.at[1, k], (q * 2 + c, x)).start()
+
+        ret[k, c, me_q] = u_send[k, me_q]
+
+    finish(0)
     whole.wait_recv()
-    second_ref[...] = sec_in[...]
-    second_ref[me_q] = sec_out[me_q]
+    sec_in[me_q] = sec_out[me_q]
+    grad[1] = sec_in[...].reshape(BLK, BLK)
+    finish(1)
+    for k in range(2):
+        u_whole(k).wait_recv()
+        u_core(k).start()
+    for k in range(2):
+        u_core(k).wait_recv()
+
+    for i in range(12):
+        for j in range(6):
+            slot = table_s[6 * i + j, 2]
+            tile = ret[lax.rem(slot, 2), lax.rem(lax.div(slot, 2), 2), lax.div(slot, 4)].astype(jnp.float32)
+            for h in range(2):
+                rows = jnp.where(c == 0, tile[8 * h : 8 * h + 4], tile[8 * h + 4 : 8 * h + 8])
+                for r in range(4):
+                    stage[r, i : i + 1, pl.ds(j * BLK + h * (BLK // 2), BLK // 2)] = rows[r : r + 1]
+
+    update_ref[...] = stage[:, 0:12, :].astype(jnp.bfloat16)
+    for k in range(2):
+        u_whole(k).wait_send()
+        u_core(k).wait_send()
+        for n in range(4):
+            fresh_out(n, k).wait()
 
     whole.wait_send()
     sec_copy.wait_send()
@@ -459,8 +606,10 @@
             hop(zb4_s, zb4_r, zb4_sem, (dy, d), z_target(d)).wait_send()
 
 
-def owner_gradients(activations, cotangent, block_owner, token_scale):
-    owner_row = jnp.pad(block_owner, (0, 56), constant_values=-1).reshape(1, 128)
+def on_device(
+    activations, cotangent, block_owner, left_factor, right_factor, left_basis, right_basis
+):
+    token_scale = 1.0 / math.sqrt(activations.shape[0] * lax.axis_size("dp"))
     i16, f32, i32, bf16 = jnp.int16, jnp.float32, jnp.int32, jnp.bfloat16
     vmem, dma = pltpu.VMEM, pltpu.SemaphoreType.DMA
 
@@ -469,17 +618,25 @@
 
     ha, hb = RA // 2 + 16, RB // 2 + 16
     fa, fb = RA + 16, RB + 16
+    whole = pl.BlockSpec(memory_space=pltpu.VMEM)
+    anywhere = pl.BlockSpec(memory_space=pl.ANY)
     return pl.pallas_call(
         functools.partial(gradient_kernel, token_scale),
-        out_shape=(
-            jax.ShapeDtypeStruct((BLK, BLK), f32),
-            jax.ShapeDtypeStruct((NQ, 8, BLK), f32),
-        ),
-        in_specs=[pl.BlockSpec(memory_space=pltpu.VMEM)] * 3,
-        out_specs=[pl.BlockSpec(memory_space=pltpu.VMEM)] * 2,
+        out_shape=(jax.ShapeDtypeStruct((4, 12, 1536), bf16),)
+        + tuple(jax.ShapeDtypeStruct((2, BLK, BLK), f32) for _ in range(4)),
+        in_specs=[whole] + [anywhere] * 6,
+        out_specs=[whole] + [anywhere] * 4,
         scratch_shapes=[
-            vmem((128, 128), i32),
-            pltpu.SMEM((128, 128), i32),
+            vmem((1, 128), i32),
+            vmem((512, 768), bf16),
+            vmem((4, 2, BLK, BLK), f32),
+            vmem((4, 2, BLK, BLK), f32),
+            vmem((2, BLK, BLK), f32),
+            vmem((2, NQ, 16, BLK // 2), bf16),
+            vmem((2, 2, NQ, 16, BLK // 2), bf16),
+            vmem((4, 16, 1536), f32),
+            vmem((136, 128), i32),
+            pltpu.SMEM((136, 128), i32),
             vmem((2, 3 * NX, BLK, 512), bf16),
             vmem((2, 6, 512, BLK), bf16),
             vmem((NZ, NY, RA + RB, BLK), f32),
@@ -513,90 +670,16 @@
             dma((2, 2)),
             dma,
             dma((4,)),
+            dma((8,)),
+            dma((4,)),
+            dma((4, 2)),
+            dma((2, 2)),
+            dma((2, 2)),
         ],
         compiler_params=pltpu.CompilerParams(
-            collective_id=0, has_side_effects=True, vmem_limit_bytes=48 * 1024 * 1024
+            collective_id=0, has_side_effects=True, vmem_limit_bytes=58 * 1024 * 1024
         ),
-    )(owner_row, activations, cotangent)
-
-
-def product(left_side, right_side):
-    return jnp.dot(left_side, right_side, precision=HIGHEST, preferred_element_type=jnp.float32)
-
-
-def orthogonalize(matrix):
-    current = matrix / jnp.sqrt(jnp.sum(matrix * matrix) + EPS)
-    identity = jnp.eye(matrix.shape[0], dtype=jnp.float32)
-    for _ in range(NSTEPS):
-        current = product(current, 1.5 * identity - 0.5 * product(current.T, current))
-    return current
-
-
-def refresh(gradient, left_old, right_old, left_prev, right_prev):
-    order_size = gradient.shape[0]
-    left_new = BETA * left_old + (1.0 - BETA) / order_size * product(gradient, gradient.T)
-    right_new = BETA * right_old + (1.0 - BETA) / order_size * product(gradient.T, gradient)
-    left_power = product(left_new, left_prev)
-    right_power = product(right_new, right_prev)
-    left_fresh = orthogonalize(left_power)
-    right_fresh = orthogonalize(right_power)
-    left_scale = (jnp.mean(left_power * left_power, axis=0) + EPS) ** (-0.125)
-    right_scale = (jnp.mean(right_power * right_power, axis=0) + EPS) ** (-0.125)
-    rotated = product(product(left_fresh.T, gradient), right_fresh)
-    rotated = rotated * left_scale[:, None] * right_scale[None, :]
-    block_update = product(product(left_fresh, rotated), right_fresh.T).astype(jnp.bfloat16)
-    return (block_update, left_new, right_new, left_fresh, right_fresh)
-
-
-def slot_numbers(block_owner, capacity):
-    positions = jnp.arange(block_owner.shape[0], dtype=jnp.int32)
-    same_owner = block_owner[:, None] == block_owner[None, :]
-    earlier = positions[None, :] < positions[:, None]
-    slot_rank = jnp.sum(jnp.where(same_owner & earlier, 1, 0), axis=1).astype(jnp.int32)
-    return block_owner * capacity + slot_rank
-
-
-def on_device(
-    activations, cotangent, block_owner, left_factor, right_factor, left_basis, right_basis
-):
-    dp_count = lax.axis_size("dp")
-    token_scale = 1.0 / math.sqrt(activations.shape[0] * dp_count)
-    slot_ids = slot_numbers(block_owner, 2)
-    primary, second = owner_gradients(activations, cotangent, block_owner, token_scale)
-    own_index = lax.axis_index("dp")
-    held = jnp.sum(jnp.where(block_owner == own_index, 1, 0))
-    live_here = jnp.stack([held > 0, held > 1])
-    owned_blocks = jnp.stack([primary, second.reshape(BLK, BLK)])
-
-    def handle_slot(unused_carry, slot_entry):
-        is_live = slot_entry[0]
-        operands = slot_entry[1:]
-
-        def refresh_slot(values):
-            return refresh(*values)
-
-        def skip_slot(values):
-            return (
-                jnp.zeros(values[0].shape, jnp.bfloat16),
-                values[1],
-                values[2],
-                values[3],
-                values[4],
-            )
-
-        return (unused_carry, lax.cond(is_live, refresh_slot, skip_slot, operands))
-
-    _, results = lax.scan(
-        handle_slot,
-        jnp.zeros((), jnp.int32),
-        (live_here, owned_blocks, left_factor, right_factor, left_basis, right_basis),
-    )
-    updates, left_next, right_next, left_basis_next, right_basis_next = results
-    outgoing = jnp.swapaxes(updates, 0, 1)
-    returned = lax.all_to_all(outgoing, "dp", split_axis=0, concat_axis=1, tiled=True)
-    own_rows = jnp.take(returned, slot_ids, axis=1)
-    update = own_rows.reshape(own_rows.shape[0], 12, 1536)
-    return (update, left_next, right_next, left_basis_next, right_basis_next)
+    )(block_owner.reshape(1, 72), activations, cotangent, left_factor, right_factor, left_basis, right_basis)
 
 
 def solution(mesh):

time: 187 us -> 118 us (0.63)
  starting transfers between devices: 32.7 us -> 0 us
  matrix products: 23.8 us -> 0 us
  Pallas kernels: 92.7 us -> 111 us
  waiting for transfers between devices: 12.7 us -> 0 us
  local copies, waits for them, and re-layouts: 18 us -> 6.11 us
  loops' own time: 3.14 us -> 0 us
    all_to_all x1 -> x0, starting transfers between devices: 32.7 us -> none  [on_device(): lax.all_to_all(outgoing, 'dp', split_axis=0, concat_axis=1, tiled=True)]
    dot_general x32 -> x0, matrix products: 23.8 us -> none  [product(): jnp.dot(left_side, right_side, precision=HIGHEST, preferred_element_type=...]
    pallas_call x1, Pallas kernels: 92.7 us -> 111 us  [on_device(): pl.pallas_call(functools.partial(gradient_kernel, token_scale), out_shape...]
    all_to_all x1 -> x0, waiting for transfers between devices: 12.7 us -> none  [on_device(): lax.all_to_all(outgoing, 'dp', split_axis=0, concat_axis=1, tiled=True)]
    dynamic_update_slice x6 -> x0, local copies, waits for them, and re-layouts: 6.7 us -> none  [on_device(): lax.scan(handle_slot, jnp.zeros((), jnp.int32), (live_here, owned_blocks,...]
    another operation x3 -> x0, loops' own time: 3.14 us -> none  [the longest x2 1.62 us: handle_slot(): return (unused_carry, lax.cond(is_live, refresh_slot, skip_slot, operands))]
    squeeze x8 -> x0, local copies, waits for them, and re-layouts: 2.92 us -> none  [on_device(): lax.scan(handle_slot, jnp.zeros((), jnp.int32), (live_here, owned_blocks,...]
    while x1 -> x0, local copies, waits for them, and re-layouts: 1.91 us -> none  [on_device(): lax.scan(handle_slot, jnp.zeros((), jnp.int32), (live_here, owned_blocks,...]
  transfers between devices with their start and end apart: 1 -> 0, of which waited for: 1 -> 0; matrix products, arithmetic and copies ran while one was open for 0% -> 0% of each run, Pallas kernels for 0% -> 0%
where the time goes in v2:
time: 118 us
  Pallas kernels  111 us (94%)
  local copies, waits for them, and re-layouts  6.11 us (5%)
    pallas_call x1, Pallas kernels, on_device(): pl.pallas_call(functools.partial(gradient_kernel, token_scale), out_shape...  111 us
    unnamed x10, local copies, waits for them, and re-layouts  4.32 us

profile of v2, /device:TPU:1, one launch (start us, length us, event | category | flops | bytes accessed | tf_op | source)
XLA Modules:
  0.0 117.9 jit_solution(7613636331737999526)
XLA Ops:
  0.6 111.2 %shard_map.110 = (bf16[4,12,1536]{2,1,0:T(8,128)(2,1)}, f32[2,256,256]{2,1,0:T(8,128)}, f32[2,256,256]{2,1,0:T(8,128)}, f32[2,256,256]{2,1,0:T(8,128)}, f32[2,256,256]{2,1,0:T(8,128)}) custom-call(s32[1,72]{1,0:T(1,128)} %bitcast.1, bf16[512,768]{1,0:T(8,128)(2,1)} %act_hbm.1, bf16[512,1536]{1,0:T(8,128)(2,1)} %cot_hbm.1, f32[2,256,256]{2,1,0:T(8,128)} %left_hbm.1, ...), custom_call_target="tpu_custom_call" | custom-call | tf_op jit(solution)/shard_map/pallas_call | solution.py:623
  111.8 0.0 copy-start.2
  111.8 0.0 copy-start.1
  111.8 1.8 %copy.12 = bf16[4,12,1536]{2,0,1:T(4,128)(2,1)} copy(bf16[4,12,1536]{2,1,0:T(8,128)(2,1)} %get-tuple-element.5) | data formatting | bytes 294912 | tf_op jit(solution)/shard_map/pallas_call | solution.py:623
  113.6 0.0 copy-start
  113.6 1.9 %copy.17 = f32[2,256,256]{2,1,0:T(8,128)} copy(f32[2,256,256]{2,1,0:T(8,128)} %get-tuple-element.16) | data formatting | bytes 1048576
  115.5 0.0 copy-done.2
  115.5 0.8 copy.18
  116.3 0.0 copy-done.1
  116.3 0.8 copy.19
  117.1 0.0 copy-done
  117.1 0.8 copy.20
Async XLA Ops:
  111.8 3.7 %copy-start.2 = (f32[2,256,256]{2,1,0:T(8,128)S(1)}, f32[2,256,256]{2,1,0:T(8,128)}, u32[]{:S(2)}) copy-start(f32[2,256,256]{2,1,0:T(8,128)} %get-tuple-element.17) | copy-start | bytes 1572868
  111.8 4.5 %copy-start.1 = (f32[2,256,256]{2,1,0:T(8,128)S(1)}, f32[2,256,256]{2,1,0:T(8,128)}, u32[]{:S(2)}) copy-start(f32[2,256,256]{2,1,0:T(8,128)} %get-tuple-element.18) | copy-start | bytes 1572868
  113.6 3.5 %copy-start = (f32[2,256,256]{2,1,0:T(8,128)S(1)}, f32[2,256,256]{2,1,0:T(8,128)}, u32[]{:S(2)}) copy-start(f32[2,256,256]{2,1,0:T(8,128)} %get-tuple-element.19) | copy-start | bytes 1572868

commit v3 on v2

v3 whole, which is shorter than its diff:
```python
import functools
import math

import jax
import jax.numpy as jnp
from jax import lax
from jax.experimental import pallas as pl
from jax.experimental.pallas import tpu as pltpu
from jax.sharding import PartitionSpec as P

NSTEPS = 6
BETA = 0.9
EPS = 1e-06
MESH = pl.DeviceIdType.MESH
NX, NY, NZ, NQ = 4, 4, 8, 32
BLK = 256
SLICES = ((64, 64), (96, 64))
SPARE = 8
PROWS = 128


def place():
    dp = lax.axis_index("dp")
    x = lax.axis_index("mp")
    return x, lax.rem(lax.div(dp, 2), NY), lax.div(dp, 2 * NY), lax.rem(dp, 2)


def device(dx=0, dy=0, dz=0, dc=0):
    x, y, z, c = place()
    x = lax.rem(x + dx + NX, NX)
    y = lax.rem(y + dy + NY, NY)
    z = lax.rem(z + dz + NZ, NZ)
    c = lax.rem(c + dc, 2)
    return ((z * NY + y) * 2 + c, x)


def remote(src, dst, send, recv, target):
    return pltpu.make_async_remote_copy(
        src_ref=src, dst_ref=dst, send_sem=send, recv_sem=recv, device_id=target, device_id_type=MESH
    )


def encode(read, groups, dst):
    exponents = []
    for g in range(groups):
        value = read(g)
        top = jnp.max(jnp.abs(value), axis=0, keepdims=True)
        exponent = jnp.ceil(jnp.log2(jnp.maximum(top, 1e-30) * (1.0 / 32700.0)))
        exponents.append(exponent)
        coded = jnp.round(value * jnp.exp2(-exponent))
        dst[pl.ds(16 * g, 16), :] = coded.astype(jnp.int32).astype(jnp.int16)
    exponents.append(jnp.zeros((16 - groups, BLK), jnp.float32))
    tile = jnp.concatenate(exponents, axis=0)
    dst[pl.ds(16 * groups, 16), :] = tile.astype(jnp.int32).astype(jnp.int16)


def decoder(src, groups):
    scales = jnp.exp2(src[pl.ds(16 * groups, 16), :].astype(jnp.int32).astype(jnp.float32))

    def read(g):
        value = src[pl.ds(16 * g, 16), :].astype(jnp.int32).astype(jnp.float32)
        return value * scales[g : g + 1, :]

    return read


def split(value):
    high = value.astype(jnp.bfloat16)
    return high, (value - high.astype(jnp.float32)).astype(jnp.bfloat16)


def turned(parts):
    return parts[0].T, parts[1].T


def times(left_parts, right_parts):
    def dot(a, b):
        return jnp.dot(a, b, preferred_element_type=jnp.float32)

    low = dot(left_parts[1], right_parts[0]) + dot(left_parts[0], right_parts[1])
    return dot(left_parts[0], right_parts[0]) + low


def refresh(gradient, held, fresh, k, live):
    def keep(n, value):
        fresh[n, k] = value if live is None else jnp.where(live, value, held[n, k])

    g = split(gradient)
    gt = turned(g)
    share = (1.0 - BETA) / BLK
    factors = [BETA * held[0, k] + share * times(g, gt), BETA * held[1, k] + share * times(gt, g)]
    powers, scales = [], []
    for n in range(2):
        keep(n, factors[n])
        power = times(split(factors[n]), split(held[2 + n, k]))
        square = jnp.sum(power * power, axis=0, keepdims=True)
        scales.append(jnp.exp(-0.125 * jnp.log(square * (1.0 / BLK) + EPS)))
        powers.append(power / jnp.sqrt(jnp.sum(square, axis=1, keepdims=True) + EPS))

    def step(_, values):
        parts = [split(v) for v in values]
        grams = [times(turned(p), p) for p in parts]
        moves = [times(p, split(gram)) for p, gram in zip(parts, grams)]
        return tuple(1.5 * v - 0.5 * m for v, m in zip(values, moves))

    bases = lax.fori_loop(0, NSTEPS, step, tuple(powers))
    weights = []
    for n in range(2):
        keep(2 + n, bases[n])
        weights.append(times(split(bases[n] * scales[n]), turned(split(bases[n]))))
    inner = times(g, split(weights[1]))
    return times(split(weights[0]), split(inner))


def gradient_kernel(
    token_scale,
    owner_ref,
    act_hbm,
    cot_hbm,
    left_hbm,
    right_hbm,
    left_basis_hbm,
    right_basis_hbm,
    slots_out,
    ret_out,
    left_out,
    right_out,
    left_basis_out,
    right_basis_out,
    owner_v,
    act_ref,
    held,
    fresh,
    grad,
    u_send,
    ret,
    table_v,
    table_s,
    at,
    cot2,
    spill,
    rings,
    sec,
    sec_out,
    sec_in,
    x_send,
    x_recv,
    f_send,
    f_recv,
    c_send,
    c_recv,
    t_sem,
    s_sem,
    in_sem,
    held_sem,
    out_sem,
    u_sem,
    r_sem,
):
    x, y, z, c = place()
    me_q = z * NY + y
    other = device(dc=1)

    def act_in(n):
        columns = pl.ds(n * 384, 384)
        return pltpu.make_async_copy(act_hbm.at[:, columns], act_ref.at[:, columns], in_sem.at[6 + n])

    def cot_in(j):
        return pltpu.make_async_copy(cot_hbm.at[:, pl.ds(j * BLK, BLK)], cot2.at[0, j], in_sem.at[j])

    factors = (left_hbm, right_hbm, left_basis_hbm, right_basis_hbm)
    results = (left_out, right_out, left_basis_out, right_basis_out)

    def held_in(n):
        return pltpu.make_async_copy(factors[n], held.at[n], held_sem.at[n])

    def fresh_out(n, k):
        return pltpu.make_async_copy(fresh.at[n, k], results[n].at[k], out_sem.at[n, k])

    act_in(0).start()
    act_in(1).start()
    for j in range(6):
        cot_in(j).start()
    for n in range(4):
        held_in(n).start()

    barrier = pltpu.get_barrier_semaphore()
    neighbours = [device(dx=1), device(dx=3), device(dy=1), device(dy=3), device(dz=1), device(dz=7), other]
    for target in neighbours:
        pl.semaphore_signal(barrier, inc=1, device_id=target, device_id_type=MESH)

    def turn(s, p):
        at[s][0, p] = act_ref[:, pl.ds(p * BLK + s * PROWS, PROWS)].T

    def own_piece(s, p, d):
        sgn = 1 - 2 * d
        return remote(
            at[s].at[0, p],
            at[s].at[0, 3 * ((4 - sgn) % 4) + p],
            x_send.at[s, d, p],
            x_recv.at[s, d, p],
            device(dx=sgn),
        )

    far = ((0, 0, 128, 0), (2, 0, 128, 1), (1, 0, 64, 0), (1, 64, 64, 1))

    def forward_piece(s, n):
        p, start, size, d = far[n]
        sgn = 1 - 2 * d
        rows = pl.ds(start, size)
        return remote(
            at[s].at[0, 3 * ((4 - sgn) % 4) + p, rows],
            at[s].at[0, 6 + p, rows],
            f_send.at[s, n],
            f_recv.at[s, n],
            device(dx=sgn),
        )

    def core_shard(s, r):
        rows = pl.ds(3 * r, 3)
        n = {0: 0, 3: 1, 1: 2}[r]
        return remote(at[s].at[0, rows], at[s].at[1, rows], c_send.at[s, n], c_recv.at[s, n], other)

    def core_piece(s, n):
        p, start, size, _ = far[n]
        rows = pl.ds(start, size)
        return remote(
            at[s].at[0, 6 + p, rows], at[s].at[1, 6 + p, rows], c_send.at[s, 3 + n], c_recv.at[s, 3 + n], other
        )

    def gather_start(s):
        for n in range(3):
            own_piece(s, n, 0).start()
            own_piece(s, 2 - n, 1).start()
        core_shard(s, 0).start()

    def gather_forward(s):
        for n in range(4):
            p, _, _, d = far[n]
            own_piece(s, p, d).wait_recv()
            forward_piece(s, n).start()
        own_piece(s, 2, 0).wait_recv()
        own_piece(s, 0, 1).wait_recv()

    def gather_share(s):
        core_shard(s, 3).start()
        core_shard(s, 1).start()

    def gather_end(s):
        for n in range(4):
            forward_piece(s, n).wait_recv()
            core_piece(s, n).start()
        for r in (0, 3, 1):
            core_shard(s, r).wait_recv()
        for n in range(4):
            core_piece(s, n).wait_recv()

    act_in(0).wait()
    act_in(1).wait()
    for p in (0, 2, 1):
        turn(0, p)
    pl.semaphore_wait(barrier, 7)
    gather_start(0)
    for j in range(6):
        cot_in(j).wait()
    cot_copy = remote(cot2.at[0], cot2.at[1], c_send.at[0, 7], c_recv.at[0, 7], other)
    cot_copy.start()
    for p in range(3):
        turn(1, p)

    owner_v[...] = jnp.full((1, 128), -1, jnp.int32)
    owner_v[:, pl.ds(0, 72)] = owner_ref[...]
    owners = owner_v[...]
    lanes = lax.broadcasted_iota(jnp.int32, (128, 128), 1)
    subs = lax.broadcasted_iota(jnp.int32, (128, 128), 0)
    earlier = lanes < subs
    owner_column = jnp.broadcast_to(owners, (128, 128)).T
    same = owner_column == owners
    is_second = jnp.max(jnp.where(same & earlier & (subs < 72), 1, 0), axis=1, keepdims=True)
    is_second = jnp.broadcast_to(is_second, (128, 128))
    second_row = is_second.T
    rank = jnp.sum(jnp.where(earlier, second_row, 0), axis=1, keepdims=True)
    rank = jnp.broadcast_to(rank, (128, 128))
    rank_row = rank.T
    mine = owners == subs
    first = jnp.min(jnp.where(mine, lanes, 71), axis=1, keepdims=True)
    entry = jnp.sum(jnp.where(mine, second_row * rank_row, 0), axis=1, keepdims=True)
    numbers = jnp.sum(jnp.where(rank == lanes, is_second * subs, 0), axis=0, keepdims=True)
    entry = jnp.minimum(entry, SPARE - 1)
    count = jnp.sum(jnp.where(mine, 1, 0), axis=1, keepdims=True)
    columns = jnp.where(lanes == 0, first, jnp.where(lanes == 1, entry, count))
    table_v[0:128, :] = columns
    table_v[128:136, :] = jnp.broadcast_to(numbers, (8, 128))
    slots_out[...] = (2 * owners + second_row[0:1, :])[:, 0:72]
    table_copy = pltpu.make_async_copy(table_v, table_s, t_sem)
    table_copy.start()
    table_copy.wait()

    gather_forward(0)
    gather_start(1)
    gather_share(0)

    def product_of(block, s):
        band = lax.rem(lax.div(block, 6) - 3 * x + 12, 12)
        column = lax.rem(block, 6)
        total = jnp.dot(at[s][0, band], cot2[0, column], preferred_element_type=jnp.float32)
        total += jnp.dot(at[s][1, band], cot2[1, column], preferred_element_type=jnp.float32)
        return total * token_scale

    def ring(s):
        ra, rb = SLICES[s]
        part = rings[s]["part"]
        wire = rings[s]["wire"]
        sems = rings[s]["sems"]

        def hop(name, index, target, rows=None):
            src, dst = wire[name]
            send, recv = sems[name].at[(0,) + index], sems[name].at[(1,) + index]
            if rows is not None:
                index = index + (pl.ds(0, rows),)
            return remote(src.at[index], dst.at[index], send, recv, target)

        def produce(dz):
            @pl.loop(0, NY)
            def _(dy):
                q = lax.rem(z + dz, NZ) * NY + lax.rem(y + dy, NY)
                part[dz, dy, pl.ds(0, PROWS), :] = product_of(table_s[2 * q + c, 0], s)

        def rows_of(dz, dy, start):
            def read(g):
                return part[dz, dy, pl.ds(start + 16 * g, 16), :]

            return read

        def joined(reads, groups):
            def read(g):
                return reads[g // groups](g % groups)

            return read

        def plus(first_read, second_read, low, high, shift=0):
            def read(g):
                if low <= g < high:
                    return first_read(g) + second_read(g - low + shift)
                return first_read(g)

            return read

        ga, gb = ra // 16, rb // 16
        pairs = {4: (4,), 3: (3, 5), 2: (2, 6), 1: (1, 7), 0: (0,)}

        def y_target(d):
            return device(dy=1 - 2 * d)

        def z_target(d):
            return device(dz=1 - 2 * d)

        def a_y2(k):
            rows = len(pairs[k]) * ra // 2 + 16
            for d in range(2):
                reads = [rows_of(dz, 2, d * (ra // 2)) for dz in pairs[k]]
                encode(joined(reads, ga // 2), len(reads) * ga // 2, wire["ya2"][0].at[k, d])
                hop("ya2", (k, d), y_target(d), rows).start()

        def a_y1(k):
            count = len(pairs[k])
            for d in range(2):
                hop("ya2", (k, d), y_target(d), count * ra // 2 + 16).wait_recv()
                arrived = decoder(wire["ya2"][1].at[k, d], count * ga // 2)
                low = d * (ga // 2)
                reads = [
                    plus(rows_of(dz, 1 + 2 * d, 0), arrived, low, low + ga // 2, n * (ga // 2))
                    for n, dz in enumerate(pairs[k])
                ]
                encode(joined(reads, ga), count * ga, wire["ya1"][0].at[k, d])
                hop("ya1", (k, d), y_target(d), count * ra + 16).start()

        def a_yf(k):
            count = len(pairs[k])
            for d in range(2):
                hop("ya1", (k, d), y_target(d), count * ra + 16).wait_recv()
            left, right = [decoder(wire["ya1"][1].at[k, d], count * ga) for d in range(2)]
            for n, dz in enumerate(pairs[k]):
                for g in range(ga):
                    part[dz, 0, pl.ds(16 * g, 16), :] += left(n * ga + g) + right(n * ga + g)

        def a_z(k):
            for d in range(2):
                dz = k if d == 0 else 8 - k
                if k == 4:
                    encode(rows_of(4, 0, d * (ra // 2)), ga // 2, wire["za4"][0].at[d])
                    hop("za4", (d,), z_target(d)).start()
                    continue
                if k == 3:
                    hop("za4", (d,), z_target(d)).wait_recv()
                    low = d * (ga // 2)
                    read = plus(rows_of(dz, 0, 0), decoder(wire["za4"][1].at[d], ga // 2), low, low + ga // 2)
                else:
                    hop("za", (k, d), z_target(d)).wait_recv()
                    read = plus(rows_of(dz, 0, 0), decoder(wire["za"][1].at[k, d], ga), 0, ga)
                encode(read, ga, wire["za"][0].at[k - 1, d])
                hop("za", (k - 1, d), z_target(d)).start()

        def b_z(k):
            @pl.loop(0, 2)
            def _(n):
                for d in range(2):
                    dz = k if d == 0 else 8 - k
                    dys = (2 - 2 * n, 3 - 2 * n)
                    if k == 4:
                        reads = [rows_of(4, dy, ra + d * (rb // 2)) for dy in dys]
                        encode(joined(reads, gb // 2), gb, wire["zb4"][0].at[n, d])
                        hop("zb4", (n, d), z_target(d)).start()
                        continue
                    if k == 3:
                        hop("zb4", (n, d), z_target(d)).wait_recv()
                        arrived = decoder(wire["zb4"][1].at[n, d], gb)
                        low, many = d * (gb // 2), gb // 2
                    else:
                        hop("zb", (k, n, d), z_target(d)).wait_recv()
                        arrived = decoder(wire["zb"][1].at[k, n, d], 2 * gb)
                        low, many = 0, gb
                    reads = [
                        plus(rows_of(dz, dy, ra), arrived, low, low + many, m * many) for m, dy in enumerate(dys)
                    ]
                    encode(joined(reads, gb), 2 * gb, wire["zb"][0].at[k - 1, n, d])
                    hop("zb", (k - 1, n, d), z_target(d)).start()

        def b_zf(n):
            for d in range(2):
                hop("zb", (0, n, d), z_target(d)).wait_recv()
            left, right = [decoder(wire["zb"][1].at[0, n, d], 2 * gb) for d in range(2)]
            for m in range(2):
                for g in range(gb):
                    part[0, 2 - 2 * n + m, pl.ds(ra + 16 * g, 16), :] += left(m * gb + g) + right(m * gb + g)

        def b_y2():
            for d in range(2):
                encode(rows_of(0, 2, ra + d * (rb // 2)), gb // 2, wire["yb2"][0].at[d])
                hop("yb2", (d,), y_target(d)).start()

        def b_y1():
            for d in range(2):
                hop("yb2", (d,), y_target(d)).wait_recv()
                low = d * (gb // 2)
                arrived = decoder(wire["yb2"][1].at[d], gb // 2)
                encode(plus(rows_of(0, 1 + 2 * d, ra), arrived, low, low + gb // 2), gb, wire["yb1"][0].at[d])
                hop("yb1", (d,), y_target(d)).start()

        def finish_b(store):
            for d in range(2):
                hop("yb1", (d,), y_target(d)).wait_recv()
            left, right = [decoder(wire["yb1"][1].at[d], gb) for d in range(2)]
            for g in range(gb):
                store(g, part[0, 0, pl.ds(ra + 16 * g, 16), :] + left(g) + right(g))

        def finish_a(store):
            for d in range(2):
                hop("za", (0, d), z_target(d)).wait_recv()
            left, right = [decoder(wire["za"][1].at[0, d], ga) for d in range(2)]
            for g in range(ga):
                store(g, part[0, 0, pl.ds(16 * g, 16), :] + left(g) + right(g))

        def phase(n):
            if n == 0:
                produce(4)
                b_z(4)
                a_y2(4)
            elif n == 1:
                produce(3)
                produce(5)
                a_y2(3)
                b_z(3)
                a_y1(4)
            elif n == 2:
                produce(2)
                produce(6)
                a_y2(2)
                a_y1(3)
                b_z(2)
                a_yf(4)
                a_z(4)
            elif n == 3:
                produce(1)
                produce(7)
                a_y2(1)
                a_y1(2)
                a_yf(3)
                a_z(3)
                b_z(1)
            elif n == 4:
                produce(0)
                a_y2(0)
                a_y1(1)
                a_yf(2)
                a_z(2)
                b_zf(0)
                b_y2()
            elif n == 5:
                a_y1(0)
                a_yf(1)
                a_z(1)
                b_zf(1)
                b_y1()
                a_yf(0)

        def drain():
            for d in range(2):
                for k in range(5):
                    hop("ya2", (k, d), y_target(d), len(pairs[k]) * ra // 2 + 16).wait_send()
                    hop("ya1", (k, d), y_target(d), len(pairs[k]) * ra + 16).wait_send()
                hop("za4", (d,), z_target(d)).wait_send()
                hop("yb2", (d,), y_target(d)).wait_send()
                hop("yb1", (d,), y_target(d)).wait_send()
                for k in range(3):
                    hop("za", (k, d), z_target(d)).wait_send()
                    for n in range(2):
                        hop("zb", (k, n, d), z_target(d)).wait_send()
                for n in range(2):
                    hop("zb4", (n, d), z_target(d)).wait_send()

        return phase, finish_a, finish_b, drain

    phase1, finish_a1, finish_b1, drain1 = ring(0)
    phase2, finish_a2, finish_b2, drain2 = ring(1)

    def second_rows(h):
        ra = SLICES[1][0]

        @pl.loop(0, SPARE // 2)
        def _(s):
            spill[...] = product_of(table_s[128, 2 * s + c], h).reshape(NQ // 2, 8, BLK)

            @pl.loop(0, NQ // 2)
            def _(r):
                q = r + h * (NQ // 2)
                dz = lax.rem(lax.div(q, NY) - z + NZ, NZ)
                dy = lax.rem(lax.rem(q, NY) - y + NY, NY)
                rings[1]["part"][dz, dy, pl.ds(pl.multiple_of(PROWS + 8 * s, 8), 8), :] = spill[r]

    def store_a1(g, rows):
        grad[0, pl.ds(16 * g, 16), :] = rows

    def store_b1(g, rows):
        grad[0, pl.ds(64 + 16 * g, 16), :] = rows

    def store_a2(g, rows):
        grad[0, pl.ds(PROWS + 16 * g, 16), :] = rows

    def store_b2(g, rows):
        if g < 2:
            grad[0, pl.ds(224 + 16 * g, 16), :] = rows
        else:
            sec[c, pl.ds(2 * (g - 2), 2)] = rows.reshape(2, 8, BLK)

    gather_end(0)
    cot_copy.wait_recv()
    phase1(0)
    phase1(1)
    second_rows(0)
    gather_forward(1)
    gather_share(1)
    phase1(2)
    phase1(3)
    gather_end(1)
    second_rows(1)
    phase2(0)
    phase1(4)
    phase2(1)
    phase1(5)
    phase2(2)
    finish_b1(store_b1)
    finish_a1(store_a1)
    phase2(3)
    phase2(4)
    phase2(5)
    finish_b2(store_b2)
    sec_copy = remote(sec.at[c], sec.at[c], s_sem.at[0], s_sem.at[1], other)
    sec_copy.start()

    finish_a2(store_a2)

    sec_copy.wait_recv()

    @pl.loop(0, NQ)
    def _(q):
        place_of = table_s[2 * q + c, 1]
        sec_out[q] = sec[lax.rem(place_of, 2), lax.div(place_of, 2)]

    @pl.loop(1, NQ)
    def _(r):
        q = lax.rem(me_q + r, NQ)
        remote(sec_out.at[q], sec_in.at[me_q], s_sem.at[2], s_sem.at[3], (q * 2 + c, x)).start()

    whole = remote(sec_out.at[pl.ds(0, NQ - 1)], sec_in.at[pl.ds(0, NQ - 1)], s_sem.at[2], s_sem.at[3], other)
    for n in range(4):
        held_in(n).wait()

    def u_whole(k):
        part_of = pl.ds(0, NQ - 1)
        return remote(u_send.at[k, part_of], ret.at[k, c, part_of], u_sem.at[0, k], u_sem.at[1, k], other)

    def u_core(k):
        return remote(ret.at[k, c], ret.at[k, c], r_sem.at[0, k], r_sem.at[1, k], other)

    def finish(k):
        update = refresh(grad[k], held, fresh, k, None if k == 0 else table_s[me_q * 2 + c, 2] > 1)
        for n in range(4):
            fresh_out(n, k).start()
        rows = update.reshape(NQ, 8, BLK)
        halves = jnp.concatenate([rows[:, :, : BLK // 2], rows[:, :, BLK // 2 :]], axis=1)
        u_send[k] = halves.astype(jnp.bfloat16)

        @pl.loop(1, NQ)
        def _(r):
            q = lax.rem(me_q + r, NQ)
            remote(u_send.at[k, q], ret.at[k, c, me_q], u_sem.at[0, k], u_sem.at[1, k], (q * 2 + c, x)).start()

        ret[k, c, me_q] = u_send[k, me_q]

    finish(0)
    whole.wait_recv()
    sec_in[me_q] = sec_out[me_q]
    grad[1] = sec_in[...].reshape(BLK, BLK)
    finish(1)
    for k in range(2):
        u_whole(k).wait_recv()
        u_core(k).start()
    for k in range(2):
        u_core(k).wait_recv()

    ret_copy = pltpu.make_async_copy(ret, ret_out, t_sem)
    ret_copy.start()
    for k in range(2):
        u_whole(k).wait_send()
        u_core(k).wait_send()
        for n in range(4):
            fresh_out(n, k).wait()

    whole.wait_send()
    sec_copy.wait_send()
    cot_copy.wait_send()
    for s in range(2):
        for r in (0, 3, 1):
            core_shard(s, r).wait_send()
        for n in range(4):
            core_piece(s, n).wait_send()
            forward_piece(s, n).wait_send()
        for p in range(3):
            own_piece(s, p, 0).wait_send()
            own_piece(s, p, 1).wait_send()
    drain1()
    drain2()
    ret_copy.wait()


def hand_over(slots, returned, results):
    def body(slot_ref, ret_hbm, *refs):
        sources, update_ref, targets = refs[:4], refs[4], refs[5:9]
        ret, held, in_sem, out_sem = refs[9:]
        core = lax.rem(lax.axis_index("dp"), 2)
        loads = [pltpu.make_async_copy(sources[n], held.at[n], in_sem.at[n]) for n in range(4)]
        stores = [pltpu.make_async_copy(held.at[n], targets[n], out_sem.at[n]) for n in range(4)]
        rows_in = pltpu.make_async_copy(ret_hbm, ret, in_sem.at[4])
        rows_in.start()
        for load in loads:
            load.start()
        for load, store in zip(loads, stores):
            load.wait()
            store.start()
        rows_in.wait()
        for i in range(12):
            for j in range(6):
                slot = slot_ref[0, 6 * i + j]
                tile = ret[lax.rem(slot, 2), lax.rem(lax.div(slot, 2), 2), lax.div(slot, 4)].astype(jnp.float32)
                for h in range(2):
                    rows = jnp.where(core == 0, tile[8 * h : 8 * h + 4], tile[8 * h + 4 : 8 * h + 8])
                    columns = pl.ds(j * BLK + h * (BLK // 2), BLK // 2)
                    update_ref[i, :, columns] = rows.astype(jnp.bfloat16)
        for store in stores:
            store.wait()

    anywhere = pl.BlockSpec(memory_space=pl.ANY)
    return pl.pallas_call(
        body,
        out_shape=(jax.ShapeDtypeStruct((12, 4, 1536), jnp.bfloat16),)
        + tuple(jax.ShapeDtypeStruct(r.shape, r.dtype) for r in results),
        in_specs=[pl.BlockSpec(memory_space=pltpu.SMEM)] + [anywhere] * 5,
        out_specs=[pl.BlockSpec(memory_space=pltpu.VMEM)] + [anywhere] * 4,
        scratch_shapes=[
            pltpu.VMEM(returned.shape, returned.dtype),
            pltpu.VMEM((4, 2, BLK, BLK), jnp.float32),
            pltpu.SemaphoreType.DMA((5,)),
            pltpu.SemaphoreType.DMA((4,)),
        ],
    )(slots, returned, *results)


def on_device(
    activations, cotangent, block_owner, left_factor, right_factor, left_basis, right_basis
):
    token_scale = 1.0 / math.sqrt(activations.shape[0] * lax.axis_size("dp"))
    i16, f32, i32, bf16 = jnp.int16, jnp.float32, jnp.int32, jnp.bfloat16
    vmem, dma = pltpu.VMEM, pltpu.SemaphoreType.DMA

    def pair(*shape):
        return (vmem(shape + (BLK,), i16), vmem(shape + (BLK,), i16))

    def ring_scratch(ra, rb):
        return dict(
            part=vmem((NZ, NY, ra + rb, BLK), f32),
            wire=dict(
                ya2=pair(5, 2, ra + 16),
                ya1=pair(5, 2, 2 * ra + 16),
                za4=pair(2, ra // 2 + 16),
                za=pair(3, 2, ra + 16),
                zb4=pair(2, 2, rb + 16),
                zb=pair(3, 2, 2, 2 * rb + 16),
                yb2=pair(2, rb // 2 + 16),
                yb1=pair(2, rb + 16),
            ),
            sems=dict(
                ya2=dma((2, 5, 2)),
                ya1=dma((2, 5, 2)),
                za4=dma((2, 2)),
                za=dma((2, 3, 2)),
                zb4=dma((2, 2, 2)),
                zb=dma((2, 3, 2, 2)),
                yb2=dma((2, 2)),
                yb1=dma((2, 2)),
            ),
        )

    whole = pl.BlockSpec(memory_space=pltpu.VMEM)
    anywhere = pl.BlockSpec(memory_space=pl.ANY)
    slots, returned, *results = pl.pallas_call(
        functools.partial(gradient_kernel, token_scale),
        out_shape=(jax.ShapeDtypeStruct((1, 72), i32), jax.ShapeDtypeStruct((2, 2, NQ, 16, BLK // 2), bf16))
        + tuple(jax.ShapeDtypeStruct((2, BLK, BLK), f32) for _ in range(4)),
        in_specs=[whole] + [anywhere] * 6,
        out_specs=[whole] + [anywhere] * 5,
        scratch_shapes=[
            vmem((1, 128), i32),
            vmem((512, 768), bf16),
            vmem((4, 2, BLK, BLK), f32),
            vmem((4, 2, BLK, BLK), f32),
            vmem((2, BLK, BLK), f32),
            vmem((2, NQ, 16, BLK // 2), bf16),
            vmem((2, 2, NQ, 16, BLK // 2), bf16),
            vmem((136, 128), i32),
            pltpu.SMEM((136, 128), i32),
            tuple(vmem((2, 3 * NX, PROWS, 512), bf16) for _ in SLICES),
            vmem((2, 6, 512, BLK), bf16),
            vmem((NQ // 2, 8, BLK), f32),
            tuple(ring_scratch(*rows) for rows in SLICES),
            vmem((2, SPARE // 2, 8, BLK), f32),
            vmem((NQ, 8, BLK), f32),
            vmem((NQ, 8, BLK), f32),
            dma((2, 2, 3)),
            dma((2, 2, 3)),
            dma((2, 4)),
            dma((2, 4)),
            dma((2, 8)),
            dma((2, 8)),
            dma,
            dma((4,)),
            dma((8,)),
            dma((4,)),
            dma((4, 2)),
            dma((2, 2)),
            dma((2, 2)),
        ],
        compiler_params=pltpu.CompilerParams(
            collective_id=0, has_side_effects=True, vmem_limit_bytes=58 * 1024 * 1024
        ),
    )(block_owner.reshape(1, 72), activations, cotangent, left_factor, right_factor, left_basis, right_basis)
    update, *results = hand_over(slots, returned, results)
    return (jnp.swapaxes(update, 0, 1), *results)


def solution(mesh):
    placed = (
        P("dp", "mp"),
        P("dp", "mp"),
        P(),
        P("dp", "mp", None),
        P("dp", "mp", None),
        P("dp", "mp", None),
        P("dp", "mp", None),
    )
    return jax.shard_map(
        on_device,
        mesh=mesh,
        in_specs=placed,
        out_specs=(
            P("dp", None, "mp"),
            P("dp", "mp", None),
            P("dp", "mp", None),
            P("dp", "mp", None),
            P("dp", "mp", None),
        ),
        check_vma=False,
    )
```

time: 118 us -> 113 us (0.958)
  local copies, waits for them, and re-layouts: 6.11 us -> 0 us
    unnamed x10 -> x0, local copies, waits for them, and re-layouts: 4.32 us -> none
    pallas_call x0 -> x1, Pallas kernels: none -> 3.91 us  [hand_over(): pl.pallas_call(body, out_shape=(jax.ShapeDtypeStruct((12, 4, 1536), jnp.b...]
    pallas_call x1, Pallas kernels: 111 us -> 108 us  [on_device(): pl.pallas_call(functools.partial(gradient_kernel, token_scale), out_shape...]
    pallas_call x1 -> x0, local copies, waits for them, and re-layouts: 1.79 us -> none  [on_device(): pl.pallas_call(functools.partial(gradient_kernel, token_scale), out_shape...]
where the time goes in v3:
time: 113 us
  Pallas kernels  112 us (99%)
    pallas_call x1, Pallas kernels, on_device(): pl.pallas_call(functools.partial(gradient_kernel, token_scale), out_shape...  108 us
    pallas_call x1, Pallas kernels, hand_over(): pl.pallas_call(body, out_shape=(jax.ShapeDtypeStruct((12, 4, 1536), jnp.b...  3.91 us

profile of v3, /device:TPU:1, one launch (start us, length us, event | category | flops | bytes accessed | tf_op | source)
XLA Modules:
  0.0 112.9 jit_solution(5241523520005342950)
XLA Ops:
  0.6 108.4 %shard_map.110 = (s32[1,72]{1,0:T(1,128)}, bf16[2,2,32,16,128]{4,3,2,1,0:T(8,128)(2,1)}, f32[2,256,256]{2,1,0:T(8,128)}, f32[2,256,256]{2,1,0:T(8,128)}, f32[2,256,256]{2,1,0:T(8,128)}, /*index=5*/f32[2,256,256]{2,1,0:T(8,128)}) custom-call(s32[1,72]{1,0:T(1,128)} %bitcast.2, bf16[512,768]{1,0:T(8,128)(2,1)} %act_hbm.1, bf16[512,1536]{1,0:T(8,128)(2,1)} %cot_hbm.1, ...), custom_call_target="tpu_custom_call" | custom-call | tf_op jit(solution)/shard_map/pallas_call | solution.py:736
  109.0 3.9 %shard_map.111 = (bf16[12,4,1536]{2,1,0:T(4,128)(2,1)}, f32[2,256,256]{2,1,0:T(8,128)}, f32[2,256,256]{2,1,0:T(8,128)}, f32[2,256,256]{2,1,0:T(8,128)}, f32[2,256,256]{2,1,0:T(8,128)}) custom-call(s32[1,72]{1,0:T(1,128)} %get-tuple-element.16.slot_ref, bf16[2,2,32,16,128]{4,3,2,1,0:T(8,128)(2,1)} %get-tuple-element.17.ret_hbm, ...), custom_call_target="tpu_custom_call" | custom-call | tf_op jit(solution)/shard_map/pallas_call | solution.py:684

commit v4 on v3

--- a/solution.py
+++ b/solution.py
@@ -17,6 +17,161 @@
 SLICES = ((64, 64), (96, 64))
 SPARE = 8
 PROWS = 128
+ORDER = (
+    ("gf", 0, 1),
+    ("gf", 0, 0),
+    ("gf", 0, 2),
+    ("gf", 0, 3),
+    ("gs", 1),
+    ("gsh", 0),
+    ("ge", 0, 1),
+    ("ge", 0, 0),
+    ("ge", 0, 2),
+    ("ge", 0, 3),
+    ("gd", 0),
+    ("sec", 0),
+    ("P", 0, 4),
+    ("gf", 1, 0),
+    ("gf", 1, 1),
+    ("AY2", 0, 4, 0),
+    ("B", 0, 4, 0, 1),
+    ("B", 0, 4, 1, 1),
+    ("B", 0, 4, 0, 0),
+    ("B", 0, 4, 1, 0),
+    ("AY2", 0, 4, 1),
+    ("P", 0, 5),
+    ("gf", 1, 2),
+    ("gf", 1, 3),
+    ("P", 0, 3),
+    ("AY2", 0, 3, 1),
+    ("AY1", 0, 4, 0),
+    ("AY2", 0, 3, 0),
+    ("P", 0, 2),
+    ("B", 0, 3, 0, 1),
+    ("B", 0, 3, 0, 0),
+    ("gsh", 1),
+    ("B", 0, 3, 1, 0),
+    ("AY1", 0, 4, 1),
+    ("B", 0, 3, 1, 1),
+    ("P", 0, 7),
+    ("P", 0, 1),
+    ("AY1", 0, 3, 1),
+    ("ge", 1, 1),
+    ("ge", 1, 0),
+    ("AY1", 0, 3, 0),
+    ("AY2", 0, 1, 0),
+    ("AY2", 0, 1, 1),
+    ("P", 0, 6),
+    ("ge", 1, 3),
+    ("ge", 1, 2),
+    ("B", 0, 2, 0, 0),
+    ("B", 0, 2, 0, 1),
+    ("AY2", 0, 2, 1),
+    ("AY2", 0, 2, 0),
+    ("AYF", 0, 4),
+    ("AZ", 0, 4, 1),
+    ("B", 0, 2, 1, 1),
+    ("AZ", 0, 4, 0),
+    ("gd", 1),
+    ("sec", 1),
+    ("P", 1, 4),
+    ("AY2", 1, 4, 0),
+    ("B", 1, 4, 0, 1),
+    ("B", 1, 4, 0, 0),
+    ("B", 1, 4, 1, 1),
+    ("AY2", 1, 4, 1),
+    ("B", 1, 4, 1, 0),
+    ("AY1", 0, 2, 0),
+    ("B", 0, 1, 0, 1),
+    ("B", 0, 2, 1, 0),
+    ("P", 1, 3),
+    ("AY1", 0, 2, 1),
+    ("P", 1, 5),
+    ("AY2", 1, 3, 0),
+    ("B", 1, 3, 0, 0),
+    ("AY1", 1, 4, 0),
+    ("AY2", 1, 3, 1),
+    ("AY1", 1, 4, 1),
+    ("B", 1, 3, 0, 1),
+    ("B", 1, 3, 1, 0),
+    ("B", 1, 3, 1, 1),
+    ("AYF", 0, 3),
+    ("AZ", 0, 3, 1),
+    ("B", 0, 1, 0, 0),
+    ("AZ", 0, 3, 0),
+    ("AY1", 0, 1, 1),
+    ("P", 1, 6),
+    ("B", 0, 1, 1, 0),
+    ("P", 1, 2),
+    ("AY1", 1, 3, 0),
+    ("AY2", 1, 2, 1),
+    ("AY2", 1, 2, 0),
+    ("AY1", 1, 3, 1),
+    ("B", 1, 2, 0, 1),
+    ("B", 1, 2, 0, 0),
+    ("AYF", 1, 4),
+    ("AZ", 1, 4, 1),
+    ("AZ", 1, 4, 0),
+    ("B", 1, 2, 1, 0),
+    ("AY1", 0, 1, 0),
+    ("B", 0, 1, 1, 1),
+    ("B", 1, 2, 1, 1),
+    ("AYF", 0, 2),
+    ("P", 1, 7),
+    ("AZ", 0, 2, 1),
+    ("P", 1, 1),
+    ("AY1", 1, 2, 1),
+    ("AY2", 1, 1, 1),
+    ("AY2", 1, 1, 0),
+    ("B", 1, 1, 0, 1),
+    ("AZ", 0, 2, 0),
+    ("P", 0, 0),
+    ("AY1", 1, 2, 0),
+    ("AYF", 1, 3),
+    ("B", 1, 1, 0, 0),
+    ("AZ", 1, 3, 1),
+    ("AY2", 0, 0, 1),
+    ("AY2", 0, 0, 0),
+    ("BF", 0, 0),
+    ("AZ", 1, 3, 0),
+    ("BY2", 0, 0),
+    ("AYF", 0, 1),
+    ("BY2", 0, 1),
+    ("BF", 0, 1),
+    ("P", 1, 0),
+    ("B", 1, 1, 1, 0),
+    ("AY2", 1, 0, 1),
+    ("AY2", 1, 0, 0),
+    ("B", 1, 1, 1, 1),
+    ("AY1", 1, 1, 0),
+    ("AZ", 0, 1, 1),
+    ("AZ", 0, 1, 0),
+    ("AY1", 1, 1, 1),
+    ("AY1", 0, 0, 1),
+    ("AYF", 1, 2),
+    ("BF", 1, 0),
+    ("BY2", 1, 0),
+    ("BY2", 1, 1),
+    ("BY1", 0, 1),
+    ("AY1", 0, 0, 0),
+    ("AZ", 1, 2, 1),
+    ("BY1", 0, 0),
+    ("AZ", 1, 2, 0),
+    ("AY1", 1, 0, 1),
+    ("AY1", 1, 0, 0),
+    ("BF", 1, 1),
+    ("AYF", 1, 1),
+    ("BY1", 1, 0),
+    ("AZ", 1, 1, 1),
+    ("AZ", 1, 1, 0),
+    ("AYF", 0, 0),
+    ("FA", 0),
+    ("BY1", 1, 1),
+    ("FB", 0),
+    ("AYF", 1, 0),
+    ("FA", 1),
+    ("FB", 1),
+)
 
 
 def place():
@@ -77,8 +232,8 @@
     def dot(a, b):
         return jnp.dot(a, b, preferred_element_type=jnp.float32)
 
-    low = dot(left_parts[1], right_parts[0]) + dot(left_parts[0], right_parts[1])
-    return dot(left_parts[0], right_parts[0]) + low
+    both = dot(jnp.concatenate(left_parts, axis=0), right_parts[0])
+    return both[:BLK] + (both[BLK:] + dot(left_parts[0], right_parts[1]))
 
 
 def refresh(gradient, held, fresh, k, live):
@@ -234,26 +389,28 @@
             own_piece(s, 2 - n, 1).start()
         core_shard(s, 0).start()
 
-    def gather_forward(s):
-        for n in range(4):
-            p, _, _, d = far[n]
-            own_piece(s, p, d).wait_recv()
-            forward_piece(s, n).start()
+    def forward(s, n):
+        p, _, _, d = far[n]
+        own_piece(s, p, d).wait_recv()
+        forward_piece(s, n).start()
+
+    def share(s):
         own_piece(s, 2, 0).wait_recv()
         own_piece(s, 0, 1).wait_recv()
-
-    def gather_share(s):
         core_shard(s, 3).start()
         core_shard(s, 1).start()
 
-    def gather_end(s):
-        for n in range(4):
-            forward_piece(s, n).wait_recv()
-            core_piece(s, n).start()
+    def pass_on(s, n):
+        forward_piece(s, n).wait_recv()
+        core_piece(s, n).start()
+
+    def gathered(s):
         for r in (0, 3, 1):
             core_shard(s, r).wait_recv()
         for n in range(4):
             core_piece(s, n).wait_recv()
+        if s == 0:
+            cot_copy.wait_recv()
 
     act_in(0).wait()
     act_in(1).wait()
@@ -296,10 +453,6 @@
     table_copy.start()
     table_copy.wait()
 
-    gather_forward(0)
-    gather_start(1)
-    gather_share(0)
-
     def product_of(block, s):
         band = lax.rem(lax.div(block, 6) - 3 * x + 12, 12)
         column = lax.rem(block, 6)
@@ -355,25 +508,23 @@
         def z_target(d):
             return device(dz=1 - 2 * d)
 
-        def a_y2(k):
+        def a_y2(k, d):
             rows = len(pairs[k]) * ra // 2 + 16
-            for d in range(2):
-                reads = [rows_of(dz, 2, d * (ra // 2)) for dz in pairs[k]]
-                encode(joined(reads, ga // 2), len(reads) * ga // 2, wire["ya2"][0].at[k, d])
-                hop("ya2", (k, d), y_target(d), rows).start()
-
-        def a_y1(k):
+            reads = [rows_of(dz, 2, d * (ra // 2)) for dz in pairs[k]]
+            encode(joined(reads, ga // 2), len(reads) * ga // 2, wire["ya2"][0].at[k, d])
+            hop("ya2", (k, d), y_target(d), rows).start()
+
+        def a_y1(k, d):
             count = len(pairs[k])
-            for d in range(2):
-                hop("ya2", (k, d), y_target(d), count * ra // 2 + 16).wait_recv()
-                arrived = decoder(wire["ya2"][1].at[k, d], count * ga // 2)
-                low = d * (ga // 2)
-                reads = [
-                    plus(rows_of(dz, 1 + 2 * d, 0), arrived, low, low + ga // 2, n * (ga // 2))
-                    for n, dz in enumerate(pairs[k])
-                ]
-                encode(joined(reads, ga), count * ga, wire["ya1"][0].at[k, d])
-                hop("ya1", (k, d), y_target(d), count * ra + 16).start()
+            hop("ya2", (k, d), y_target(d), count * ra // 2 + 16).wait_recv()
+            arrived = decoder(wire["ya2"][1].at[k, d], count * ga // 2)
+            low = d * (ga // 2)
+            reads = [
+                plus(rows_of(dz, 1 + 2 * d, 0), arrived, low, low + ga // 2, n * (ga // 2))
+                for n, dz in enumerate(pairs[k])
+            ]
+            encode(joined(reads, ga), count * ga, wire["ya1"][0].at[k, d])
+            hop("ya1", (k, d), y_target(d), count * ra + 16).start()
 
         def a_yf(k):
             count = len(pairs[k])
@@ -384,47 +535,41 @@
                 for g in range(ga):
                     part[dz, 0, pl.ds(16 * g, 16), :] += left(n * ga + g) + right(n * ga + g)
 
-        def a_z(k):
-            for d in range(2):
-                dz = k if d == 0 else 8 - k
-                if k == 4:
-                    encode(rows_of(4, 0, d * (ra // 2)), ga // 2, wire["za4"][0].at[d])
-                    hop("za4", (d,), z_target(d)).start()
-                    continue
-                if k == 3:
-                    hop("za4", (d,), z_target(d)).wait_recv()
-                    low = d * (ga // 2)
-                    read = plus(rows_of(dz, 0, 0), decoder(wire["za4"][1].at[d], ga // 2), low, low + ga // 2)
-                else:
-                    hop("za", (k, d), z_target(d)).wait_recv()
-                    read = plus(rows_of(dz, 0, 0), decoder(wire["za"][1].at[k, d], ga), 0, ga)
-                encode(read, ga, wire["za"][0].at[k - 1, d])
-                hop("za", (k - 1, d), z_target(d)).start()
-
-        def b_z(k):
-            @pl.loop(0, 2)
-            def _(n):
-                for d in range(2):
-                    dz = k if d == 0 else 8 - k
-                    dys = (2 - 2 * n, 3 - 2 * n)
-                    if k == 4:
-                        reads = [rows_of(4, dy, ra + d * (rb // 2)) for dy in dys]
-                        encode(joined(reads, gb // 2), gb, wire["zb4"][0].at[n, d])
-                        hop("zb4", (n, d), z_target(d)).start()
-                        continue
-                    if k == 3:
-                        hop("zb4", (n, d), z_target(d)).wait_recv()
-                        arrived = decoder(wire["zb4"][1].at[n, d], gb)
-                        low, many = d * (gb // 2), gb // 2
-                    else:
-                        hop("zb", (k, n, d), z_target(d)).wait_recv()
-                        arrived = decoder(wire["zb"][1].at[k, n, d], 2 * gb)
-                        low, many = 0, gb
-                    reads = [
-                        plus(rows_of(dz, dy, ra), arrived, low, low + many, m * many) for m, dy in enumerate(dys)
-                    ]
-                    encode(joined(reads, gb), 2 * gb, wire["zb"][0].at[k - 1, n, d])
-                    hop("zb", (k - 1, n, d), z_target(d)).start()
+        def a_z(k, d):
+            dz = k if d == 0 else 8 - k
+            if k == 4:
+                encode(rows_of(4, 0, d * (ra // 2)), ga // 2, wire["za4"][0].at[d])
+                hop("za4", (d,), z_target(d)).start()
+                return
+            if k == 3:
+                hop("za4", (d,), z_target(d)).wait_recv()
+                low = d * (ga // 2)
+                read = plus(rows_of(dz, 0, 0), decoder(wire["za4"][1].at[d], ga // 2), low, low + ga // 2)
+            else:
+                hop("za", (k, d), z_target(d)).wait_recv()
+                read = plus(rows_of(dz, 0, 0), decoder(wire["za"][1].at[k, d], ga), 0, ga)
+            encode(read, ga, wire["za"][0].at[k - 1, d])
+            hop("za", (k - 1, d), z_target(d)).start()
+
+        def b_z(k, n, d):
+            dz = k if d == 0 else 8 - k
+            dys = (2 - 2 * n, 3 - 2 * n)
+            if k == 4:
+                reads = [rows_of(4, dy, ra + d * (rb // 2)) for dy in dys]
+                encode(joined(reads, gb // 2), gb, wire["zb4"][0].at[n, d])
+                hop("zb4", (n, d), z_target(d)).start()
+                return
+            if k == 3:
+                hop("zb4", (n, d), z_target(d)).wait_recv()
+                arrived = decoder(wire["zb4"][1].at[n, d], gb)
+                low, many = d * (gb // 2), gb // 2
+            else:
+                hop("zb", (k, n, d), z_target(d)).wait_recv()
+                arrived = decoder(wire["zb"][1].at[k, n, d], 2 * gb)
+                low, many = 0, gb
+            reads = [plus(rows_of(dz, dy, ra), arrived, low, low + many, m * many) for m, dy in enumerate(dys)]
+            encode(joined(reads, gb), 2 * gb, wire["zb"][0].at[k - 1, n, d])
+            hop("zb", (k - 1, n, d), z_target(d)).start()
 
         def b_zf(n):
             for d in range(2):
@@ -434,75 +579,30 @@
                 for g in range(gb):
                     part[0, 2 - 2 * n + m, pl.ds(ra + 16 * g, 16), :] += left(m * gb + g) + right(m * gb + g)
 
-        def b_y2():
-            for d in range(2):
-                encode(rows_of(0, 2, ra + d * (rb // 2)), gb // 2, wire["yb2"][0].at[d])
-                hop("yb2", (d,), y_target(d)).start()
-
-        def b_y1():
-            for d in range(2):
-                hop("yb2", (d,), y_target(d)).wait_recv()
-                low = d * (gb // 2)
-                arrived = decoder(wire["yb2"][1].at[d], gb // 2)
-                encode(plus(rows_of(0, 1 + 2 * d, ra), arrived, low, low + gb // 2), gb, wire["yb1"][0].at[d])
-                hop("yb1", (d,), y_target(d)).start()
-
-        def finish_b(store):
+        def b_y2(d):
+            encode(rows_of(0, 2, ra + d * (rb // 2)), gb // 2, wire["yb2"][0].at[d])
+            hop("yb2", (d,), y_target(d)).start()
+
+        def b_y1(d):
+            hop("yb2", (d,), y_target(d)).wait_recv()
+            low = d * (gb // 2)
+            arrived = decoder(wire["yb2"][1].at[d], gb // 2)
+            encode(plus(rows_of(0, 1 + 2 * d, ra), arrived, low, low + gb // 2), gb, wire["yb1"][0].at[d])
+            hop("yb1", (d,), y_target(d)).start()
+
+        def finish_b():
             for d in range(2):
                 hop("yb1", (d,), y_target(d)).wait_recv()
             left, right = [decoder(wire["yb1"][1].at[d], gb) for d in range(2)]
             for g in range(gb):
-                store(g, part[0, 0, pl.ds(ra + 16 * g, 16), :] + left(g) + right(g))
-
-        def finish_a(store):
+                store_b(s, g, part[0, 0, pl.ds(ra + 16 * g, 16), :] + left(g) + right(g))
+
+        def finish_a():
             for d in range(2):
                 hop("za", (0, d), z_target(d)).wait_recv()
             left, right = [decoder(wire["za"][1].at[0, d], ga) for d in range(2)]
             for g in range(ga):
-                store(g, part[0, 0, pl.ds(16 * g, 16), :] + left(g) + right(g))
-
-        def phase(n):
-            if n == 0:
-                produce(4)
-                b_z(4)
-                a_y2(4)
-            elif n == 1:
-                produce(3)
-                produce(5)
-                a_y2(3)
-                b_z(3)
-                a_y1(4)
-            elif n == 2:
-                produce(2)
-                produce(6)
-                a_y2(2)
-                a_y1(3)
-                b_z(2)
-                a_yf(4)
-                a_z(4)
-            elif n == 3:
-                produce(1)
-                produce(7)
-                a_y2(1)
-                a_y1(2)
-                a_yf(3)
-                a_z(3)
-                b_z(1)
-            elif n == 4:
-                produce(0)
-                a_y2(0)
-                a_y1(1)
-                a_yf(2)
-                a_z(2)
-                b_zf(0)
-                b_y2()
-            elif n == 5:
-                a_y1(0)
-                a_yf(1)
-                a_z(1)
-                b_zf(1)
-                b_y1()
-                a_yf(0)
+                grad[0, pl.ds(PROWS * s + 16 * g, 16), :] = part[0, 0, pl.ds(16 * g, 16), :] + left(g) + right(g)
 
         def drain():
             for d in range(2):
@@ -519,10 +619,26 @@
                 for n in range(2):
                     hop("zb4", (n, d), z_target(d)).wait_send()
 
-        return phase, finish_a, finish_b, drain
-
-    phase1, finish_a1, finish_b1, drain1 = ring(0)
-    phase2, finish_a2, finish_b2, drain2 = ring(1)
+        return {
+            "P": produce,
+            "AY2": a_y2,
+            "AY1": a_y1,
+            "AYF": a_yf,
+            "AZ": a_z,
+            "B": b_z,
+            "BF": b_zf,
+            "BY2": b_y2,
+            "BY1": b_y1,
+            "FB": finish_b,
+            "FA": finish_a,
+            "drain": drain,
+        }
+
+    def store_b(s, g, rows):
+        if s == 0 or g < 2:
+            grad[0, pl.ds(PROWS * s + SLICES[s][0] + 16 * g, 16), :] = rows
+        else:
+            sec[c, pl.ds(2 * (g - 2), 2)] = rows.reshape(2, 8, BLK)
 
     def second_rows(h):
         ra = SLICES[1][0]
@@ -538,47 +654,19 @@
                 dy = lax.rem(lax.rem(q, NY) - y + NY, NY)
                 rings[1]["part"][dz, dy, pl.ds(pl.multiple_of(PROWS + 8 * s, 8), 8), :] = spill[r]
 
-    def store_a1(g, rows):
-        grad[0, pl.ds(16 * g, 16), :] = rows
-
-    def store_b1(g, rows):
-        grad[0, pl.ds(64 + 16 * g, 16), :] = rows
-
-    def store_a2(g, rows):
-        grad[0, pl.ds(PROWS + 16 * g, 16), :] = rows
-
-    def store_b2(g, rows):
-        if g < 2:
-            grad[0, pl.ds(224 + 16 * g, 16), :] = rows
-        else:
-            sec[c, pl.ds(2 * (g - 2), 2)] = rows.reshape(2, 8, BLK)
-
-    gather_end(0)
-    cot_copy.wait_recv()
-    phase1(0)
-    phase1(1)
-    second_rows(0)
-    gather_forward(1)
-    gather_share(1)
-    phase1(2)
-    phase1(3)
-    gather_end(1)
-    second_rows(1)
-    phase2(0)
-    phase1(4)
-    phase2(1)
-    phase1(5)
-    phase2(2)
-    finish_b1(store_b1)
-    finish_a1(store_a1)
-    phase2(3)
-    phase2(4)
-    phase2(5)
-    finish_b2(store_b2)
+    tasks = [ring(0), ring(1)]
+    gather = {
+        "gs": gather_start,
+        "gf": forward,
+        "gsh": share,
+        "ge": pass_on,
+        "gd": gathered,
+        "sec": second_rows,
+    }
+    for name, s, *rest in ORDER:
+        (gather[name] if name in gather else tasks[s][name])(*(([s] if name in gather else []) + rest))
     sec_copy = remote(sec.at[c], sec.at[c], s_sem.at[0], s_sem.at[1], other)
     sec_copy.start()
-
-    finish_a2(store_a2)
 
     sec_copy.wait_recv()
 
@@ -649,8 +737,8 @@
         for p in range(3):
             own_piece(s, p, 0).wait_send()
             own_piece(s, p, 1).wait_send()
-    drain1()
-    drain2()
+    tasks[0]["drain"]()
+    tasks[1]["drain"]()
     ret_copy.wait()
 
 

time: 113 us -> 106 us (0.938)
  Pallas kernels: 112 us -> 105 us
    pallas_call x1, Pallas kernels: 108 us -> 101 us  [on_device(): pl.pallas_call(functools.partial(gradient_kernel, token_scale), out_shape...]
where the time goes in v4:
time: 106 us
  Pallas kernels  105 us (99%)
    pallas_call x1, Pallas kernels, on_device(): pl.pallas_call(functools.partial(gradient_kernel, token_scale), out_shape...  101 us
    pallas_call x1, Pallas kernels, hand_over(): pl.pallas_call(body, out_shape=(jax.ShapeDtypeStruct((12, 4, 1536), jnp.b...  3.91 us

profile of v4, /device:TPU:1, one launch (start us, length us, event | category | flops | bytes accessed | tf_op | source)
XLA Modules:
  0.0 105.9 jit_solution(14300447089730450972)
XLA Ops:
  0.6 101.4 %shard_map.110 = (s32[1,72]{1,0:T(1,128)}, bf16[2,2,32,16,128]{4,3,2,1,0:T(8,128)(2,1)}, f32[2,256,256]{2,1,0:T(8,128)}, f32[2,256,256]{2,1,0:T(8,128)}, f32[2,256,256]{2,1,0:T(8,128)}, /*index=5*/f32[2,256,256]{2,1,0:T(8,128)}) custom-call(s32[1,72]{1,0:T(1,128)} %bitcast.2, bf16[512,768]{1,0:T(8,128)(2,1)} %act_hbm.1, bf16[512,1536]{1,0:T(8,128)(2,1)} %cot_hbm.1, ...), custom_call_target="tpu_custom_call" | custom-call | tf_op jit(solution)/shard_map/pallas_call | solution.py:824
  102.0 3.9 %shard_map.111 = (bf16[12,4,1536]{2,1,0:T(4,128)(2,1)}, f32[2,256,256]{2,1,0:T(8,128)}, f32[2,256,256]{2,1,0:T(8,128)}, f32[2,256,256]{2,1,0:T(8,128)}, f32[2,256,256]{2,1,0:T(8,128)}) custom-call(s32[1,72]{1,0:T(1,128)} %get-tuple-element.16.slot_ref, bf16[2,2,32,16,128]{4,3,2,1,0:T(8,128)(2,1)} %get-tuple-element.17.ret_hbm, ...), custom_call_target="tpu_custom_call" | custom-call | tf_op jit(solution)/shard_map/pallas_call | solution.py:772

commit v5 on v4

--- a/solution.py
+++ b/solution.py
@@ -20,8 +20,8 @@
 ORDER = (
     ("gf", 0, 1),
     ("gf", 0, 0),
+    ("gf", 0, 3),
     ("gf", 0, 2),
-    ("gf", 0, 3),
     ("gs", 1),
     ("gsh", 0),
     ("ge", 0, 1),
@@ -29,148 +29,150 @@
     ("ge", 0, 2),
     ("ge", 0, 3),
     ("gd", 0),
+    ("P", 0, 4),
+    ("AY2", 0, 4, 0),
+    ("B", 0, 4, 0, 0),
+    ("B", 0, 4, 0, 1),
+    ("AY2", 0, 4, 1),
+    ("gf", 1, 1),
+    ("B", 0, 4, 1, 0),
+    ("B", 0, 4, 1, 1),
+    ("P", 0, 2),
+    ("P", 0, 5),
+    ("gf", 1, 0),
+    ("P", 0, 3),
+    ("AY2", 0, 3, 0),
+    ("gf", 1, 2),
+    ("B", 0, 3, 0, 0),
+    ("B", 0, 3, 0, 1),
+    ("AY1", 0, 4, 1),
     ("sec", 0),
-    ("P", 0, 4),
-    ("gf", 1, 0),
-    ("gf", 1, 1),
-    ("AY2", 0, 4, 0),
-    ("B", 0, 4, 0, 1),
-    ("B", 0, 4, 1, 1),
-    ("B", 0, 4, 0, 0),
-    ("B", 0, 4, 1, 0),
-    ("AY2", 0, 4, 1),
-    ("P", 0, 5),
-    ("gf", 1, 2),
     ("gf", 1, 3),
-    ("P", 0, 3),
     ("AY2", 0, 3, 1),
     ("AY1", 0, 4, 0),
-    ("AY2", 0, 3, 0),
-    ("P", 0, 2),
-    ("B", 0, 3, 0, 1),
-    ("B", 0, 3, 0, 0),
+    ("B", 0, 3, 1, 0),
     ("gsh", 1),
-    ("B", 0, 3, 1, 0),
-    ("AY1", 0, 4, 1),
+    ("P", 0, 1),
+    ("AY1", 0, 3, 0),
     ("B", 0, 3, 1, 1),
-    ("P", 0, 7),
-    ("P", 0, 1),
-    ("AY1", 0, 3, 1),
+    ("P", 0, 6),
     ("ge", 1, 1),
     ("ge", 1, 0),
-    ("AY1", 0, 3, 0),
-    ("AY2", 0, 1, 0),
-    ("AY2", 0, 1, 1),
-    ("P", 0, 6),
-    ("ge", 1, 3),
+    ("P", 0, 7),
+    ("AY2", 0, 2, 1),
     ("ge", 1, 2),
-    ("B", 0, 2, 0, 0),
-    ("B", 0, 2, 0, 1),
-    ("AY2", 0, 2, 1),
-    ("AY2", 0, 2, 0),
     ("AYF", 0, 4),
     ("AZ", 0, 4, 1),
-    ("B", 0, 2, 1, 1),
-    ("AZ", 0, 4, 0),
+    ("ge", 1, 3),
+    ("B", 0, 2, 1, 0),
+    ("AY2", 0, 2, 0),
+    ("B", 0, 2, 0, 0),
+    ("AY2", 0, 1, 0),
+    ("B", 0, 2, 0, 1),
+    ("AY1", 0, 3, 1),
     ("gd", 1),
-    ("sec", 1),
     ("P", 1, 4),
     ("AY2", 1, 4, 0),
+    ("sec", 1),
+    ("AZ", 0, 4, 0),
     ("B", 1, 4, 0, 1),
+    ("B", 1, 4, 1, 1),
     ("B", 1, 4, 0, 0),
-    ("B", 1, 4, 1, 1),
+    ("P", 1, 3),
+    ("B", 1, 4, 1, 0),
     ("AY2", 1, 4, 1),
-    ("B", 1, 4, 1, 0),
+    ("P", 1, 5),
+    ("AY2", 1, 3, 1),
+    ("P", 1, 2),
+    ("B", 1, 3, 0, 1),
+    ("AY1", 1, 4, 0),
+    ("AY2", 0, 1, 1),
+    ("B", 1, 3, 0, 0),
+    ("B", 1, 3, 1, 1),
+    ("AY2", 1, 3, 0),
+    ("AY1", 1, 4, 1),
     ("AY1", 0, 2, 0),
-    ("B", 0, 1, 0, 1),
-    ("B", 0, 2, 1, 0),
-    ("P", 1, 3),
-    ("AY1", 0, 2, 1),
-    ("P", 1, 5),
-    ("AY2", 1, 3, 0),
-    ("B", 1, 3, 0, 0),
-    ("AY1", 1, 4, 0),
-    ("AY2", 1, 3, 1),
-    ("AY1", 1, 4, 1),
-    ("B", 1, 3, 0, 1),
+    ("P", 1, 6),
+    ("AY2", 1, 2, 1),
+    ("AYF", 0, 3),
     ("B", 1, 3, 1, 0),
-    ("B", 1, 3, 1, 1),
-    ("AYF", 0, 3),
+    ("B", 0, 2, 1, 1),
+    ("AY1", 1, 3, 1),
+    ("AY2", 1, 2, 0),
     ("AZ", 0, 3, 1),
-    ("B", 0, 1, 0, 0),
     ("AZ", 0, 3, 0),
-    ("AY1", 0, 1, 1),
-    ("P", 1, 6),
-    ("B", 0, 1, 1, 0),
-    ("P", 1, 2),
-    ("AY1", 1, 3, 0),
-    ("AY2", 1, 2, 1),
-    ("AY2", 1, 2, 0),
-    ("AY1", 1, 3, 1),
-    ("B", 1, 2, 0, 1),
+    ("P", 1, 1),
     ("B", 1, 2, 0, 0),
     ("AYF", 1, 4),
+    ("B", 1, 2, 0, 1),
+    ("AY1", 1, 3, 0),
+    ("AZ", 1, 4, 0),
+    ("AY1", 0, 2, 1),
+    ("AY1", 0, 1, 1),
+    ("B", 1, 2, 1, 1),
+    ("P", 1, 7),
+    ("AY2", 1, 1, 0),
+    ("B", 0, 1, 1, 0),
+    ("P", 1, 0),
     ("AZ", 1, 4, 1),
-    ("AZ", 1, 4, 0),
+    ("AY2", 1, 0, 0),
+    ("AY2", 1, 0, 1),
     ("B", 1, 2, 1, 0),
+    ("B", 0, 1, 0, 1),
+    ("AY1", 1, 2, 0),
+    ("AY2", 1, 1, 1),
+    ("AY1", 1, 2, 1),
     ("AY1", 0, 1, 0),
+    ("B", 1, 1, 0, 0),
+    ("AYF", 0, 2),
+    ("AYF", 1, 3),
+    ("B", 1, 1, 0, 1),
+    ("P", 0, 0),
+    ("B", 0, 1, 0, 0),
+    ("AZ", 1, 3, 1),
+    ("B", 1, 1, 1, 1),
+    ("AY2", 0, 0, 1),
+    ("AZ", 1, 3, 0),
+    ("AY2", 0, 0, 0),
+    ("AY1", 1, 1, 0),
+    ("B", 1, 1, 1, 0),
+    ("AY1", 1, 1, 1),
+    ("AZ", 0, 2, 0),
+    ("BF", 1, 0),
     ("B", 0, 1, 1, 1),
-    ("B", 1, 2, 1, 1),
-    ("AYF", 0, 2),
-    ("P", 1, 7),
     ("AZ", 0, 2, 1),
-    ("P", 1, 1),
-    ("AY1", 1, 2, 1),
-    ("AY2", 1, 1, 1),
-    ("AY2", 1, 1, 0),
-    ("B", 1, 1, 0, 1),
-    ("AZ", 0, 2, 0),
-    ("P", 0, 0),
-    ("AY1", 1, 2, 0),
-    ("AYF", 1, 3),
-    ("B", 1, 1, 0, 0),
-    ("AZ", 1, 3, 1),
-    ("AY2", 0, 0, 1),
-    ("AY2", 0, 0, 0),
+    ("BY2", 1, 0),
+    ("BY2", 1, 1),
     ("BF", 0, 0),
-    ("AZ", 1, 3, 0),
+    ("BY2", 0, 1),
     ("BY2", 0, 0),
-    ("AYF", 0, 1),
-    ("BY2", 0, 1),
-    ("BF", 0, 1),
-    ("P", 1, 0),
-    ("B", 1, 1, 1, 0),
-    ("AY2", 1, 0, 1),
-    ("AY2", 1, 0, 0),
-    ("B", 1, 1, 1, 1),
-    ("AY1", 1, 1, 0),
-    ("AZ", 0, 1, 1),
-    ("AZ", 0, 1, 0),
-    ("AY1", 1, 1, 1),
+    ("AY1", 0, 0, 0),
     ("AY1", 0, 0, 1),
     ("AYF", 1, 2),
-    ("BF", 1, 0),
-    ("BY2", 1, 0),
-    ("BY2", 1, 1),
-    ("BY1", 0, 1),
-    ("AY1", 0, 0, 0),
+    ("AZ", 1, 2, 0),
     ("AZ", 1, 2, 1),
-    ("BY1", 0, 0),
-    ("AZ", 1, 2, 0),
     ("AY1", 1, 0, 1),
     ("AY1", 1, 0, 0),
+    ("AYF", 1, 1),
+    ("BY1", 1, 1),
     ("BF", 1, 1),
-    ("AYF", 1, 1),
     ("BY1", 1, 0),
+    ("BF", 0, 1),
+    ("AYF", 0, 1),
+    ("BY1", 0, 1),
+    ("AZ", 0, 1, 0),
+    ("BY1", 0, 0),
+    ("AZ", 0, 1, 1),
     ("AZ", 1, 1, 1),
     ("AZ", 1, 1, 0),
+    ("FB", 1),
+    ("sx", 1),
     ("AYF", 0, 0),
+    ("AYF", 1, 0),
     ("FA", 0),
-    ("BY1", 1, 1),
     ("FB", 0),
-    ("AYF", 1, 0),
+    ("sw", 1),
     ("FA", 1),
-    ("FB", 1),
 )
 
 
@@ -332,17 +334,14 @@
     def fresh_out(n, k):
         return pltpu.make_async_copy(fresh.at[n, k], results[n].at[k], out_sem.at[n, k])
 
+    barrier = pltpu.get_barrier_semaphore()
     act_in(0).start()
     act_in(1).start()
-    for j in range(6):
-        cot_in(j).start()
-    for n in range(4):
-        held_in(n).start()
-
-    barrier = pltpu.get_barrier_semaphore()
     neighbours = [device(dx=1), device(dx=3), device(dy=1), device(dy=3), device(dz=1), device(dz=7), other]
     for target in neighbours:
         pl.semaphore_signal(barrier, inc=1, device_id=target, device_id_type=MESH)
+    for j in range(6):
+        cot_in(j).start()
 
     def turn(s, p):
         at[s][0, p] = act_ref[:, pl.ds(p * BLK + s * PROWS, PROWS)].T
@@ -418,6 +417,8 @@
         turn(0, p)
     pl.semaphore_wait(barrier, 7)
     gather_start(0)
+    for n in range(4):
+        held_in(n).start()
     for j in range(6):
         cot_in(j).wait()
     cot_copy = remote(cot2.at[0], cot2.at[1], c_send.at[0, 7], c_recv.at[0, 7], other)
@@ -654,6 +655,24 @@
                 dy = lax.rem(lax.rem(q, NY) - y + NY, NY)
                 rings[1]["part"][dz, dy, pl.ds(pl.multiple_of(PROWS + 8 * s, 8), 8), :] = spill[r]
 
+    sec_copy = remote(sec.at[c], sec.at[c], s_sem.at[0], s_sem.at[1], other)
+
+    def second_share(_):
+        sec_copy.start()
+
+    def second_send(_):
+        sec_copy.wait_recv()
+
+        @pl.loop(0, NQ, unroll=True)
+        def _(q):
+            place_of = table_s[2 * q + c, 1]
+            sec_out[q] = sec[lax.rem(place_of, 2), lax.div(place_of, 2)]
+
+        @pl.loop(1, NQ, unroll=True)
+        def _(r):
+            q = lax.rem(me_q + r, NQ)
+            remote(sec_out.at[q], sec_in.at[me_q], s_sem.at[2], s_sem.at[3], (q * 2 + c, x)).start()
+
     tasks = [ring(0), ring(1)]
     gather = {
         "gs": gather_start,
@@ -662,24 +681,11 @@
         "ge": pass_on,
         "gd": gathered,
         "sec": second_rows,
+        "sx": second_share,
+        "sw": second_send,
     }
     for name, s, *rest in ORDER:
         (gather[name] if name in gather else tasks[s][name])(*(([s] if name in gather else []) + rest))
-    sec_copy = remote(sec.at[c], sec.at[c], s_sem.at[0], s_sem.at[1], other)
-    sec_copy.start()
-
-    sec_copy.wait_recv()
-
-    @pl.loop(0, NQ)
-    def _(q):
-        place_of = table_s[2 * q + c, 1]
-        sec_out[q] = sec[lax.rem(place_of, 2), lax.div(place_of, 2)]
-
-    @pl.loop(1, NQ)
-    def _(r):
-        q = lax.rem(me_q + r, NQ)
-        remote(sec_out.at[q], sec_in.at[me_q], s_sem.at[2], s_sem.at[3], (q * 2 + c, x)).start()
-
     whole = remote(sec_out.at[pl.ds(0, NQ - 1)], sec_in.at[pl.ds(0, NQ - 1)], s_sem.at[2], s_sem.at[3], other)
     for n in range(4):
         held_in(n).wait()
@@ -699,7 +705,7 @@
         halves = jnp.concatenate([rows[:, :, : BLK // 2], rows[:, :, BLK // 2 :]], axis=1)
         u_send[k] = halves.astype(jnp.bfloat16)
 
-        @pl.loop(1, NQ)
+        @pl.loop(1, NQ, unroll=True)
         def _(r):
             q = lax.rem(me_q + r, NQ)
             remote(u_send.at[k, q], ret.at[k, c, me_q], u_sem.at[0, k], u_sem.at[1, k], (q * 2 + c, x)).start()

time: 106 us -> 103 us (0.972)
  Pallas kernels: 105 us -> 102 us
    pallas_call x1, Pallas kernels: 101 us -> 98.1 us  [on_device(): pl.pallas_call(functools.partial(gradient_kernel, token_scale), out_shape...]
where the time goes in v5:
time: 103 us
  Pallas kernels  102 us (99%)
    pallas_call x1, Pallas kernels, on_device(): pl.pallas_call(functools.partial(gradient_kernel, token_scale), out_shape...  98.1 us
    pallas_call x1, Pallas kernels, hand_over(): pl.pallas_call(body, out_shape=(jax.ShapeDtypeStruct((12, 4, 1536), jnp.b...  3.91 us

profile of v5, /device:TPU:1, one launch (start us, length us, event | category | flops | bytes accessed | tf_op | source)
XLA Modules:
  0.0 102.8 jit_solution(14288231446940891124)
XLA Ops:
  0.6 98.1 %shard_map.110 = (s32[1,72]{1,0:T(1,128)}, bf16[2,2,32,16,128]{4,3,2,1,0:T(8,128)(2,1)}, f32[2,256,256]{2,1,0:T(8,128)}, f32[2,256,256]{2,1,0:T(8,128)}, f32[2,256,256]{2,1,0:T(8,128)}, /*index=5*/f32[2,256,256]{2,1,0:T(8,128)}) custom-call(s32[1,72]{1,0:T(1,128)} %bitcast.2, bf16[512,768]{1,0:T(8,128)(2,1)} %act_hbm.1, bf16[512,1536]{1,0:T(8,128)(2,1)} %cot_hbm.1, ...), custom_call_target="tpu_custom_call" | custom-call | tf_op jit(solution)/shard_map/pallas_call | solution.py:830
  98.7 3.9 %shard_map.111 = (bf16[12,4,1536]{2,1,0:T(4,128)(2,1)}, f32[2,256,256]{2,1,0:T(8,128)}, f32[2,256,256]{2,1,0:T(8,128)}, f32[2,256,256]{2,1,0:T(8,128)}, f32[2,256,256]{2,1,0:T(8,128)}) custom-call(s32[1,72]{1,0:T(1,128)} %get-tuple-element.16.slot_ref, bf16[2,2,32,16,128]{4,3,2,1,0:T(8,128)(2,1)} %get-tuple-element.17.ret_hbm, ...), custom_call_target="tpu_custom_call" | custom-call | tf_op jit(solution)/shard_map/pallas_call | solution.py:778

commit v6 on v5

--- a/solution.py
+++ b/solution.py
@@ -475,7 +475,7 @@
             return remote(src.at[index], dst.at[index], send, recv, target)
 
         def produce(dz):
-            @pl.loop(0, NY)
+            @pl.loop(0, NY, unroll=True)
             def _(dy):
                 q = lax.rem(z + dz, NZ) * NY + lax.rem(y + dy, NY)
                 part[dz, dy, pl.ds(0, PROWS), :] = product_of(table_s[2 * q + c, 0], s)
@@ -644,11 +644,11 @@
     def second_rows(h):
         ra = SLICES[1][0]
 
-        @pl.loop(0, SPARE // 2)
+        @pl.loop(0, SPARE // 2, unroll=2)
         def _(s):
             spill[...] = product_of(table_s[128, 2 * s + c], h).reshape(NQ // 2, 8, BLK)
 
-            @pl.loop(0, NQ // 2)
+            @pl.loop(0, NQ // 2, unroll=True)
             def _(r):
                 q = r + h * (NQ // 2)
                 dz = lax.rem(lax.div(q, NY) - z + NZ, NZ)

time: 103 us -> 101 us (0.981)
  Pallas kernels: 102 us -> 100 us
    pallas_call x1, Pallas kernels: 98.1 us -> 96.5 us  [on_device(): pl.pallas_call(functools.partial(gradient_kernel, token_scale), out_shape...]
where the time goes in v6:
time: 101 us
  Pallas kernels  100 us (99%)
    pallas_call x1, Pallas kernels, on_device(): pl.pallas_call(functools.partial(gradient_kernel, token_scale), out_shape...  96.5 us
    pallas_call x1, Pallas kernels, hand_over(): pl.pallas_call(body, out_shape=(jax.ShapeDtypeStruct((12, 4, 1536), jnp.b...  3.91 us

profile of v6, /device:TPU:1, one launch (start us, length us, event | category | flops | bytes accessed | tf_op | source)
XLA Modules:
  0.0 101.2 jit_solution(16250894984988052376)
XLA Ops:
  0.6 96.5 %shard_map.110 = (s32[1,72]{1,0:T(1,128)}, bf16[2,2,32,16,128]{4,3,2,1,0:T(8,128)(2,1)}, f32[2,256,256]{2,1,0:T(8,128)}, f32[2,256,256]{2,1,0:T(8,128)}, f32[2,256,256]{2,1,0:T(8,128)}, /*index=5*/f32[2,256,256]{2,1,0:T(8,128)}) custom-call(s32[1,72]{1,0:T(1,128)} %bitcast.2, bf16[512,768]{1,0:T(8,128)(2,1)} %act_hbm.1, bf16[512,1536]{1,0:T(8,128)(2,1)} %cot_hbm.1, ...), custom_call_target="tpu_custom_call" | custom-call | tf_op jit(solution)/shard_map/pallas_call | solution.py:830
  97.1 3.9 %shard_map.111 = (bf16[12,4,1536]{2,1,0:T(4,128)(2,1)}, f32[2,256,256]{2,1,0:T(8,128)}, f32[2,256,256]{2,1,0:T(8,128)}, f32[2,256,256]{2,1,0:T(8,128)}, f32[2,256,256]{2,1,0:T(8,128)}) custom-call(s32[1,72]{1,0:T(1,128)} %get-tuple-element.16.slot_ref, bf16[2,2,32,16,128]{4,3,2,1,0:T(8,128)(2,1)} %get-tuple-element.17.ret_hbm, ...), custom_call_target="tpu_custom_call" | custom-call | tf_op jit(solution)/shard_map/pallas_call | solution.py:778
